TPU v7x, 32 devices: a whole 2x2x4 slice. The times are simulated.
32 devices in a mesh: grp: 4 (over x, core), own: 8 (over z, y).
Axes of the slice: x: 2, y: 2, z: 4, core: 2. Of those that a mesh axis runs over, the one named last changes fastest.
Arguments:
- features: float32 [32768, 1024], P(('grp', 'own')), may hold values from -9 to 9, as said below
- targets: float32 [32768, 256], P(('grp', 'own')), may hold values from -6 to 6
- centres: float32 [1024, 1024], P('own'), may hold values from -6 to 6
- widths: float32 [1024], P('own'), may hold values from 256 to 1024
- coefficients: float32 [1024, 256], P('own'), may hold values from -0.75 to 0.75
Outputs:
- residual: float32 [32768, 256], P(('grp', 'own'))
- gradient: float32 [1024, 256], P('own')
Inputs may be any that keep to these rules, and one draw needn't show every extreme that they name: Every row of features lies near one of the centres; which centre it is is not promised.
All inputs are finite; a program needn't handle non-finite values.
Results may differ from a plain program's by a relative error of at most 0.00015.
Values sent between devices are 32-bit elements; how exact they have to be, the bound alone decides.
No kernel may reach another device: no remote copies, remote signals or barrier semaphores. Data moves between devices by JAX's collectives and lax.ppermute only.
A program may use at most 128 MiB of HBM per device.

v0:
```python
import jax
import jax.numpy as jnp
from jax import lax
from jax.sharding import PartitionSpec as P


def body(features, targets, centres, widths, coefficients):
    row_count = features.shape[0]
    owners = lax.axis_size("own")
    total_rows = row_count * lax.axis_size("grp") * owners
    row_sq = jnp.sum(features * features, axis=1)
    cen_piece = lax.all_gather(centres, "own", axis=0, tiled=True)
    width_piece = lax.all_gather(widths, "own", axis=0, tiled=True)
    coef_piece = lax.all_gather(coefficients, "own", axis=0, tiled=True)
    cross = jnp.dot(
        features, cen_piece.T, precision=lax.Precision.HIGHEST, preferred_element_type=jnp.float32
    )
    cen_sq = jnp.sum(cen_piece * cen_piece, axis=1)
    sq_dist = row_sq[:, None] + cen_sq[None, :] - 2.0 * cross
    tile = jnp.exp(-sq_dist / (2.0 * width_piece[None, :]))
    predicted = jnp.dot(
        tile, coef_piece, precision=lax.Precision.HIGHEST, preferred_element_type=jnp.float32
    )
    kernel = tile
    predicted, kernel = (predicted, kernel)
    residual = predicted - targets
    factor = 1.0 / jnp.sqrt(jnp.float32(total_rows))
    summed = lax.psum(
        lax.dot_general(
            kernel,
            residual,
            (((0,), (0,)), ((), ())),
            precision=lax.Precision.HIGHEST,
            preferred_element_type=jnp.float32,
        )
        * factor,
        "grp",
    )
    gradient = lax.psum_scatter(summed, "own", scatter_dimension=0, tiled=True)
    return (residual, gradient)


def solution(mesh):
    return jax.shard_map(
        body,
        mesh=mesh,
        in_specs=(
            P(("grp", "own"), None),
            P(("grp", "own"), None),
            P("own", None),
            P("own"),
            P("own", None),
        ),
        out_specs=(P(("grp", "own"), None), P("own", None)),
        check_vma=False,
    )
```

profile of v0, /device:TPU:0, one launch (start us, length us, event | category | flops | bytes accessed | tf_op | source)
XLA Modules:
  0.0 243.6 jit_solution(9454420617745806265)
XLA Ops:
  7.2 0.0 all-gather.4.cloned.1.call-start
  7.2 0.7 all-gather.4.cloned.1.call-update
  7.9 0.0 all-gather.6.cloned.1.call-start
  7.9 0.7 all-gather.6.cloned.1.call-update
  8.6 0.0 reduce-scatter.2.cloned.1.call-start
  8.7 22.4 %all-gather = f32[8,1,128]{2,1,0:T(1,128)S(1)} all-gather(f32[1,1,128]{2,1,0:T(1,128)} %bitcast.9), channel_id=1, replica_groups=mesh['grp'=4,'own'=8] {'own'}, dimensions={0}, use_global_device_ids=true | all-gather | bytes 4608 | tf_op jit(solution)/shard_map/all_gather | solution.py:13
  31.1 2.6 %multiply_reduce_fusion.1 = f32[1024]{0:T(1024)S(1)} fusion(f32[1024,1024]{1,0:T(8,128)} %param.5), kind=kLoop, calls=%fused_computation.2 | loop fusion | flops 2096128 | bytes 4198400 | tf_op jit(solution)/shard_map/reduce_sum | solution.py:11
  33.7 52.6 %all-gather.4.cloned.1.call-done = f32[1024,1024]{1,0:T(8,128)} async-done(((f32[128,1024]{1,0:T(8,128)}), f32[1024,1024]{1,0:T(8,128)}) %all-gather.4.cloned.1.call-update) | async-done | bytes 4194320 | tf_op jit(solution)/shard_map/all_gather | solution.py:12
  86.3 2.7 %multiply_reduce_fusion = f32[1024]{0:T(1024)S(1)} fusion(f32[1024,1024]{1,0:T(8,128)} %all-gather.4.cloned.1.call-done), kind=kLoop, calls=%fused_computation.1 | loop fusion | flops 2096128 | bytes 4198400 | tf_op jit(solution)/shard_map/reduce_sum | solution.py:18
  88.9 0.8 copy-done.1
  89.7 17.0 %divide_exponential_fusion = f32[1024,1024]{1,0:T(8,128)} fusion(f32[1024,1024]{1,0:T(8,128)S(1)} %copy-done.1, f32[1024,1024]{1,0:T(8,128)} %all-gather.4.cloned.1.call-done, f32[1024]{0:T(1024)S(1)} %bitcast.8, f32[1024]{0:T(1024)S(1)} %multiply_reduce_fusion, f32[1024]{0:T(1024)S(1)} %multiply_reduce_fusion.1), kind=kOutput, calls=%fused_computation | convolution fusion | flops 12890144768 | bytes 12595200 | tf_op jit(solution)/shard_map/dot_general | solution.py:15
  106.7 20.1 %all-gather.6.cloned.1.call-done = f32[1024,256]{1,0:T(8,128)} async-done(((f32[128,256]{1,0:T(8,128)}), f32[1024,256]{1,0:T(8,128)}) %all-gather.6.cloned.1.call-update) | async-done | bytes 1048592 | tf_op jit(solution)/shard_map/all_gather | solution.py:14
  126.8 0.0 copy-done.3
  126.8 5.8 %convolution_subtract_fusion = f32[1024,256]{1,0:T(8,128)S(1)} fusion(f32[1024,256]{1,0:T(8,128)S(1)} %copy-done.3, f32[1024,1024]{1,0:T(8,128)} %divide_exponential_fusion, f32[1024,256]{1,0:T(8,128)} %all-gather.6.cloned.1.call-done), kind=kOutput, calls=%fused_computation.4 | convolution fusion | flops 3221487616 | bytes 7340032 | tf_op jit(solution)/shard_map/dot_general | solution.py:21
  132.7 0.0 copy-done
  132.7 0.0 copy-start.2
  132.7 7.8 %convolution_multiply_fusion = f32[1024,256]{1,0:T(8,128)} fusion(f32[1024,1024]{1,0:T(8,128)S(1)} %copy-done, f32[1024,256]{1,0:T(8,128)S(1)} %convolution_subtract_fusion), kind=kOutput, calls=%fused_computation.3 | convolution fusion | flops 3221487616 | bytes 6291456 | tf_op jit(solution)/shard_map/dot_general | solution.py:29
  140.5 0.0 reduce-scatter.2.cloned.1.call-update
  140.6 0.0 all-reduce.2.cloned.1.call-start
  140.6 62.2 %reduce-scatter.2.cloned.1.call-done = f32[128,256]{1,0:T(8,128)} async-done(((f32[1024,256]{1,0:T(8,128)}), f32[128,256]{1,0:T(8,128)}) %reduce-scatter.2.cloned.1.call-update) | async-done | bytes 131088 | tf_op jit(solution)/shard_map/reduce_scatter | solution.py:39
  202.8 0.0 all-reduce.2.cloned.1.call-update
  202.8 32.7 %all-reduce.2.cloned.1.call-done = f32[128,256]{1,0:T(8,128)} async-done(((f32[128,256]{1,0:T(8,128)}), f32[128,256]{1,0:T(8,128)}) %all-reduce.2.cloned.1.call-update) | async-done | bytes 131088 | tf_op jit(solution)/shard_map/psum | solution.py:28
  235.5 1.6 copy.8
  237.1 0.0 copy-done.2
  (4 shorter events, 0.0 us)
Async XLA Ops:
  7.2 79.1 %all-gather.4.cloned.1.call-start = ((), (), s32[]{:S(2)}) async-start(), calls=%async_computation.1 | async-start | bytes 4718592 | tf_op jit(solution)/shard_map/all_gather | solution.py:12
  7.9 118.9 %all-gather.6.cloned.1.call-start = ((), (), s32[]{:S(2)}) async-start(), calls=%async_computation.2 | async-start | bytes 1179648 | tf_op jit(solution)/shard_map/all_gather | solution.py:14
  8.6 194.1 %reduce-scatter.2.cloned.1.call-start = ((), (), s32[]{:S(2)}) async-start(), calls=%async_computation.3 | async-start | bytes 1179648 | tf_op jit(solution)/shard_map/reduce_scatter | solution.py:39
  86.3 3.4 %copy-start.1 = (f32[1024,1024]{1,0:T(8,128)S(1)}, f32[1024,1024]{1,0:T(8,128)}, u32[]{:S(2)}) copy-start(f32[1024,1024]{1,0:T(8,128)} %param.5) | copy-start | bytes 12582916
  89.7 37.1 %copy-start.3 = (f32[1024,256]{1,0:T(8,128)S(1)}, f32[1024,256]{1,0:T(8,128)}, u32[]{:S(2)}) copy-start(f32[1024,256]{1,0:T(8,128)} %param.6) | copy-start | bytes 3145732
  126.8 5.8 %copy-start = (f32[1024,1024]{1,0:T(8,128)S(1)}, f32[1024,1024]{1,0:T(8,128)}, u32[]{:S(2)}) copy-start(f32[1024,1024]{1,0:T(8,128)} %divide_exponential_fusion) | copy-start | bytes 12582916
  132.7 104.4 %copy-start.2 = (f32[1024,256]{1,0:T(8,128)}, f32[1024,256]{1,0:T(8,128)S(1)}, u32[]{:S(2)}) copy-start(f32[1024,256]{1,0:T(8,128)S(1)} %convolution_subtract_fusion) | copy-start | bytes 3145732
  140.6 95.0 %all-reduce.2.cloned.1.call-start = ((), (), s32[]{:S(2)}) async-start(), calls=%async_computation.4 | async-start | bytes 262144 | tf_op jit(solution)/shard_map/psum | solution.py:28
Sparse Core Ops, SparseCore 0:
  10.1 76.0 all-gather.3
  88.4 38.4 all-gather.5
  140.7 62.0 reduce-scatter.1
  205.1 30.4 all-reduce.1
where the time goes:
time: 244 us
  waiting for transfers between devices  169 us (69%)
  matrix products  30.7 us (13%)
  blocking collectives  22.4 us (9%)
  between operations  13.8 us (6%)
  other arithmetic  5.24 us (2%)
    reduce_scatter x1, waiting for transfers between devices, body(): gradient = lax.psum_scatter(summed, 'own', scatter_dimension=0, tiled=True)  62.2 us
    all_gather x1, waiting for transfers between devices, body(): cen_piece = lax.all_gather(centres, 'own', axis=0, tiled=True)  52.6 us
    psum x1, waiting for transfers between devices, body(): lax.psum(lax.dot_general(kernel, residual, (((0,), (0,)), ((), ())), prec...  32.7 us
    all_gather x1, blocking collectives, body(): width_piece = lax.all_gather(widths, 'own', axis=0, tiled=True)  22.4 us
    all_gather x1, waiting for transfers between devices, body(): coef_piece = lax.all_gather(coefficients, 'own', axis=0, tiled=True)  20.1 us
    dot_general x1, matrix products, body(): jnp.dot(features, cen_piece.T, precision=lax.Precision.HIGHEST, preferred...  17 us
    dot_general x1, matrix products, body(): lax.dot_general(kernel, residual, (((0,), (0,)), ((), ())), precision=lax...  7.84 us
    dot_general x1, matrix products, body(): jnp.dot(tile, coef_piece, precision=lax.Precision.HIGHEST, preferred_elem...  5.83 us
  transfers between devices with their start and end apart: 4, of which 4 were waited for; matrix products, arithmetic and copies ran while one was open for 9% of the time, Pallas kernels for 0%

commit v1 on v0

v1 whole, which is shorter than its diff:
```python
import functools

import jax
import jax.numpy as jnp
from jax import lax
from jax.experimental import pallas as pl
from jax.experimental.pallas import tpu as pltpu
from jax.sharding import PartitionSpec as P

LANES = 128
F32 = jnp.float32
BF16 = jnp.bfloat16
NT = (((1,), (1,)), ((), ()))
NN = (((1,), (0,)), ((), ()))


def params():
    return pltpu.CompilerParams(vmem_limit_bytes=48 * 1024 * 1024)


def split(value):
    high = value.astype(BF16)
    return high, (value - high.astype(F32)).astype(BF16)


def mm(a, b, dims):
    return lax.dot_general(a, b, dims, preferred_element_type=F32)


def pack_kernel(parts, core_ref, cen_ref, coef_ref, width_ref, mine_ref, sib_ref, col_ref):
    count, depth = cen_ref.shape
    half = count // 2
    piece = half // parts
    col_ref[...] = jnp.transpose(jnp.broadcast_to(1.0 / width_ref[...], (count, count)))
    outs = (mine_ref, sib_ref)
    cols, squares = [], []
    for which in range(2):
        half_of = core_ref[0] if which == 0 else 1 - core_ref[0]
        out = outs[which]
        for part in range(parts):
            rows = pl.ds(pl.multiple_of(part * half + half_of * piece, piece), piece)
            total = jnp.zeros((piece, LANES), F32)
            at = part * piece
            for block in range(depth // LANES):
                value = cen_ref[rows, block * LANES:(block + 1) * LANES]
                out[block * half + at:block * half + at + piece, :] = value
                total = total + value * value
            base = half * (depth // LANES)
            for block in range(coef_ref.shape[1] // LANES):
                out[base + block * half + at:base + block * half + at + piece, :] = coef_ref[
                    rows, block * LANES:(block + 1) * LANES
                ]
            cols.append(col_ref[rows, :])
            squares.append(total)
    inverse = jnp.transpose(jnp.concatenate(cols, axis=0))[:1]
    square = 0.5 * jnp.sum(jnp.transpose(jnp.concatenate(squares, axis=0)), axis=0, keepdims=True)
    tail = mine_ref.shape[0] - 8
    for which in range(2):
        if which == 1:
            inverse = jnp.concatenate([inverse[:, half:], inverse[:, :half]], axis=1)
            square = jnp.concatenate([square[:, half:], square[:, :half]], axis=1)
        outs[which][tail:, :] = jnp.concatenate([inverse, square] + [jnp.zeros((6, LANES), F32)], axis=0)


def pack(core, centres, coefficients, widths, parts):
    count, depth = centres.shape
    rows = count // 2 * ((depth + coefficients.shape[1]) // LANES) + 8
    shape = jax.ShapeDtypeStruct((rows, LANES), F32)
    vmem = pl.BlockSpec(memory_space=pltpu.VMEM)
    return pl.pallas_call(
        functools.partial(pack_kernel, parts),
        out_shape=(shape, shape),
        in_specs=[pl.BlockSpec(memory_space=pltpu.SMEM), vmem, vmem, vmem],
        out_specs=(vmem, vmem),
        scratch_shapes=[pltpu.VMEM((count, LANES), F32)],
        compiler_params=params(),
        name="pack",
    )(core, centres, coefficients, widths)


def prep_kernel(feat_ref, tgt_ref, high_ref, low_ref, sq_ref, acc_ref):
    value = feat_ref[...]
    high, low = split(value)
    high_ref[...] = high
    low_ref[...] = low
    square = value * value
    total = square[:, :LANES]
    for block in range(1, value.shape[1] // LANES):
        total = total + square[:, block * LANES:(block + 1) * LANES]
    row = 0.5 * jnp.sum(jnp.transpose(total), axis=0, keepdims=True)
    sq_ref[...] = jnp.broadcast_to(row, sq_ref.shape)
    acc_ref[...] = -jnp.transpose(tgt_ref[...])


def prep(features, targets, step):
    rows, depth = features.shape
    width = targets.shape[1]
    return pl.pallas_call(
        prep_kernel,
        grid=(rows // step,),
        out_shape=(
            jax.ShapeDtypeStruct((rows, depth), BF16),
            jax.ShapeDtypeStruct((rows, depth), BF16),
            jax.ShapeDtypeStruct((8, rows), F32),
            jax.ShapeDtypeStruct((width, rows), F32),
        ),
        in_specs=[pl.BlockSpec((step, depth), lambda i: (i, 0)), pl.BlockSpec((step, width), lambda i: (i, 0))],
        out_specs=(
            pl.BlockSpec((step, depth), lambda i: (i, 0)),
            pl.BlockSpec((step, depth), lambda i: (i, 0)),
            pl.BlockSpec((8, step), lambda i: (0, i)),
            pl.BlockSpec((width, step), lambda i: (0, i)),
        ),
        compiler_params=params(),
        cost_estimate=pl.CostEstimate(flops=4 * rows * depth, bytes_accessed=10 * rows * depth, transcendentals=0),
        name="prep",
    )(features, targets)


def plane_kernel(half, depth, width, *refs):
    messages = refs[:4]
    fh_ref, fl_ref, sq_ref, acc_ref, kh_ref, kl_ref, out_ref, cen_ref, tmp_ref, coef_ref, inv_ref, cs_ref = refs[4:]
    count = 4 * half

    @pl.when(pl.program_id(0) == 0)
    def _():
        for q, message in enumerate(messages):
            at = q * half
            for block in range(depth // LANES):
                high, low = split(message[block * half:(block + 1) * half, :])
                lanes = slice(block * LANES, (block + 1) * LANES)
                cen_ref[at:at + half, lanes] = high
                cen_ref[count + at:count + at + half, lanes] = low
            base = half * (depth // LANES)
            for block in range(width // LANES):
                tmp_ref[at:at + half, block * LANES:(block + 1) * LANES] = message[
                    base + block * half:base + (block + 1) * half, :
                ]
            tail = half * ((depth + width) // LANES)
            for row, into in ((0, inv_ref), (1, cs_ref)):
                line = message[tail + row:tail + row + 1, :]
                into[at:at + half, :] = jnp.transpose(jnp.broadcast_to(line, (LANES, LANES)))[:half]
        high, low = split(jnp.transpose(tmp_ref[...]))
        coef_ref[:width, :] = high
        coef_ref[width:, :] = low

    fh = fh_ref[...]
    both = mm(cen_ref[...], fh, NT)
    cross = both[:count] + both[count:] + mm(cen_ref[:count, :], fl_ref[...], NT)
    shape = cross.shape
    wide = shape[1] // LANES
    cs = jnp.concatenate([cs_ref[...]] * wide, axis=1)
    inv = jnp.concatenate([inv_ref[...]] * wide, axis=1)
    value = jnp.exp((cross - cs - sq_ref[:1, :]) * inv)
    kh, kl = split(value)
    kh_ref[...] = kh
    kl_ref[...] = kl
    both = mm(coef_ref[...], kh, NN)
    out_ref[...] = acc_ref[...] + (both[:width] + both[width:] + mm(coef_ref[:width, :], kl, NN))


def plane(messages, fh, fl, sq, acc, half, step):
    rows, depth = fh.shape
    width = acc.shape[0]
    count = 4 * half
    whole = pl.BlockSpec(messages[0].shape, lambda i: (0, 0))
    block = pl.BlockSpec((step, depth), lambda i: (i, 0))
    tile = pl.BlockSpec((count, step), lambda i: (0, i))
    accs = pl.BlockSpec((width, step), lambda i: (0, i))
    return pl.pallas_call(
        functools.partial(plane_kernel, half, depth, width),
        grid=(rows // step,),
        out_shape=(
            jax.ShapeDtypeStruct((count, rows), BF16),
            jax.ShapeDtypeStruct((count, rows), BF16),
            jax.ShapeDtypeStruct((width, rows), F32),
        ),
        in_specs=[whole] * 4 + [block, block, pl.BlockSpec((8, step), lambda i: (0, i)), accs],
        out_specs=(tile, tile, accs),
        scratch_shapes=[
            pltpu.VMEM((2 * count, depth), BF16),
            pltpu.VMEM((count, width), F32),
            pltpu.VMEM((2 * width, count), BF16),
            pltpu.VMEM((count, LANES), F32),
            pltpu.VMEM((count, LANES), F32),
        ],
        compiler_params=params(),
        cost_estimate=pl.CostEstimate(
            flops=6 * rows * count * (depth + width), bytes_accessed=10 * rows * depth, transcendentals=rows * count
        ),
        name="plane",
    )(*messages, fh, fl, sq, acc)


def grad_kernel(planes, acc_ref, *refs):
    kh_refs, kl_refs, out_ref = refs[:planes], refs[planes:2 * planes], refs[2 * planes]
    high, low = split(acc_ref[...])
    for k in range(planes):
        kh = kh_refs[k][...]
        out_ref[k] = mm(kh, high, NT) + mm(kh, low, NT) + mm(kl_refs[k][...], high, NT)


def grad(acc, khs, kls, which):
    width, rows = acc.shape
    count = khs[0].shape[0] // 2
    planes = len(khs)
    tile = pl.BlockSpec((count, rows), lambda i: (which, 0))
    return pl.pallas_call(
        functools.partial(grad_kernel, planes),
        grid=(1,),
        out_shape=jax.ShapeDtypeStruct((planes, count, width), F32),
        in_specs=[pl.BlockSpec((width, rows), lambda i: (0, 0))] + [tile] * (2 * planes),
        out_specs=pl.BlockSpec((planes, count, width), lambda i: (0, 0, 0)),
        compiler_params=params(),
        cost_estimate=pl.CostEstimate(
            flops=6 * rows * count * width * planes, bytes_accessed=4 * rows * (width + count * planes), transcendentals=0
        ),
        name="grad",
    )(acc, *khs, *kls)


def body(groups, owners, features, targets, centres, widths, coefficients):
    rows, depth = features.shape
    width = targets.shape[1]
    count = centres.shape[0]
    half = count // 2
    parts = groups // 2
    deep = owners // 2
    me = lax.axis_index("grp")
    core, part = me % 2, me // 2

    def by_core(value):
        return lax.ppermute(value, "grp", [(g, g ^ 1) for g in range(groups)])

    def by_y(value):
        return lax.ppermute(value, "own", [(o, o ^ 1) for o in range(owners)])

    def by_z(value, k):
        return lax.ppermute(value, "own", [(o, (o + 2 * k) % owners) for o in range(owners)])

    mine, sib = pack(core.reshape(1), centres, coefficients, widths.reshape(1, count), parts)
    fh, fl, sq, acc = prep(features, targets, 256)
    near = by_y(mine)
    far = [by_z(mine, k) for k in range(1, deep)]
    step = min(rows, 256)
    khs, kls = [], []
    for k in range(deep):
        if k == 0:
            same, other = mine, near
            messages = (mine, near, sib, by_core(near))
        else:
            same = far[k - 1]
            other = by_y(same)
            messages = (same, other, by_core(same), by_core(other))
        kh, kl, acc = plane(messages, fh, fl, sq, acc, half, step)
        khs.append(kh)
        kls.append(kl)

    sent = by_core(grad(acc, khs, kls, 1))
    kept = grad(acc, khs, kls, 0)
    residual = jnp.transpose(acc)
    piece = half // parts
    total = (sent + kept).reshape(deep, 2, parts, piece, width)
    owned = None
    for ahead in range(parts):
        for other in range(2):
            block = lax.dynamic_index_in_dim(total[:, other], (part + ahead) % parts, 1, keepdims=False)
            if ahead or other:
                pairs = []
                for g in range(groups):
                    for o in range(owners):
                        to = ((g // 2 + ahead) % parts) * 2 + g % 2
                        pairs.append((g * owners + o, to * owners + (o ^ other)))
                block = lax.ppermute(block, ("grp", "own"), pairs)
            owned = block if owned is None else owned + block
    factor = 1.0 / jnp.sqrt(F32(rows * groups * owners))
    gradient = owned[0]
    for k in range(1, deep):
        gradient = gradient + by_z(owned[k], -k)
    gradient = lax.all_gather(gradient * factor, "grp", axis=0, tiled=True)
    return residual, gradient


def solution(mesh):
    return jax.shard_map(
        functools.partial(body, mesh.shape["grp"], mesh.shape["own"]),
        mesh=mesh,
        in_specs=(
            P(("grp", "own"), None),
            P(("grp", "own"), None),
            P("own", None),
            P("own"),
            P("own", None),
        ),
        out_specs=(P(("grp", "own"), None), P("own", None)),
        check_vma=False,
    )
```

time: 244 us -> 110 us (0.45)
  waiting for transfers between devices: 169 us -> 26.5 us
  Pallas kernels: 0 us -> 35.2 us
  matrix products: 30.7 us -> 0 us
  starting transfers between devices: 0.16 us -> 28.7 us
  blocking collectives: 22.4 us -> 5.43 us
  between operations: 13.8 us -> 0.85 us
  local copies, waits for them, and re-layouts: 2.35 us -> 11.4 us
  other arithmetic: 5.24 us -> 1.16 us
    all_gather x2 -> x0, waiting for transfers between devices: 72.7 us -> none  [the longest x1 52.6 us: body(): cen_piece = lax.all_gather(centres, 'own', axis=0, tiled=True)]
    reduce_scatter x1 -> x0, waiting for transfers between devices: 62.2 us -> none  [body(): gradient = lax.psum_scatter(summed, 'own', scatter_dimension=0, tiled=True)]
    pallas_call x0 -> x8, Pallas kernels: none -> 35.2 us  [the longest x4 25.4 us: plane(): pl.pallas_call(functools.partial(plane_kernel, half, depth, width), grid=...]
    psum x1 -> x0, waiting for transfers between devices: 32.7 us -> none  [body(): lax.psum(lax.dot_general(kernel, residual, (((0,), (0,)), ((), ())), prec...]
    dot_general x3 -> x0, matrix products: 30.7 us -> none  [the longest x1 17 us: body(): jnp.dot(features, cen_piece.T, precision=lax.Precision.HIGHEST, preferred...]
    ppermute x0 -> x21, starting transfers between devices: none -> 28.7 us  [the longest x6 18.1 us: by_z(): lax.ppermute(value, 'own', [(o, (o + 2 * k) % owners) for o in range(owne...]
    ppermute x0 -> x21, waiting for transfers between devices: none -> 26.5 us  [the longest x6 19.4 us: by_z(): lax.ppermute(value, 'own', [(o, (o + 2 * k) % owners) for o in range(owne...]
    all_gather x1, blocking collectives: 22.4 us -> 5.43 us  [body(): gradient = lax.all_gather(gradient * factor, 'grp', axis=0, tiled=True)]
  transfers between devices with their start and end apart: 4 -> 21, of which waited for: 4 -> 7; matrix products, arithmetic and copies ran while one was open for 9% -> 1% of each run, Pallas kernels for 0% -> 23%
where the time goes in v1:
time: 110 us; the launch traced here: 109 us
  Pallas kernels  35.2 us (32%)
  starting transfers between devices  28.7 us (26%)
  waiting for transfers between devices  26.5 us (24%)
  local copies, waits for them, and re-layouts  11.4 us (10%)
  blocking collectives  5.43 us (5%)
  other arithmetic  1.16 us (1%)
    pallas_call x4, Pallas kernels, plane(): pl.pallas_call(functools.partial(plane_kernel, half, depth, width), grid=...  25.4 us
    ppermute x6, waiting for transfers between devices, by_z(): lax.ppermute(value, 'own', [(o, (o + 2 * k) % owners) for o in range(owne...  19.4 us
    ppermute x6, starting transfers between devices, by_z(): lax.ppermute(value, 'own', [(o, (o + 2 * k) % owners) for o in range(owne...  18.1 us
    unnamed x28, local copies, waits for them, and re-layouts  11.3 us
    ppermute x3, waiting for transfers between devices, body(): block = lax.ppermute(block, ('grp', 'own'), pairs)  6.01 us
    all_gather x1, blocking collectives, body(): gradient = lax.all_gather(gradient * factor, 'grp', axis=0, tiled=True)  5.43 us
    ppermute x4, starting transfers between devices, by_y(): return lax.ppermute(value, 'own', [(o, o ^ 1) for o in range(owners)])  5.31 us
    pallas_call x2, Pallas kernels, grad(): pl.pallas_call(functools.partial(grad_kernel, planes), grid=(1,), out_sha...  5.03 us
  transfers between devices with their start and end apart: 21, of which 7 were waited for; matrix products, arithmetic and copies ran while one was open for 1% of the time, Pallas kernels for 23%

profile of v1, /device:TPU:0, one launch (start us, length us, event | category | flops | bytes accessed | tf_op | source)
XLA Modules:
  0.0 109.1 jit_solution(15241081359006688986)
XLA Ops:
  3.5 3.0 %collective-permute-start.8 = (f32[648,128]{1,0:T(8,128)S(1)}, f32[648,128]{1,0:T(8,128)S(1)}, u32[]{:S(2)}, u32[]{:S(2)}) collective-permute-start(f32[648,128]{1,0:T(8,128)S(1)} %get-tuple-element.20.refs_0_), channel_id=1, source_target_pairs={{0,2},{1,3},{2,4},{3,5},{4,6},{5,7},{6,0},{7,1},{8,10},{9,11},{10,... | collective-permute-start | bytes 995336 | tf_op jit(solution)/shard_map/ppermute | solution.py:239
  6.5 1.5 %collective-permute-start.12 = (f32[648,128]{1,0:T(8,128)S(1)}, f32[648,128]{1,0:T(8,128)S(1)}, u32[]{:S(2)}, u32[]{:S(2)}) collective-permute-start(f32[648,128]{1,0:T(8,128)S(1)} %get-tuple-element.20.refs_0_), channel_id=1, source_target_pairs={{0,1},{1,0},{2,3},{3,2},{4,5},{5,4},{6,7},{7,6},{8,9},{9,8},{10,11... | collective-permute-start | bytes 995336 | tf_op jit(solution)/shard_map/ppermute | solution.py:236
  8.0 2.6 %collective-permute-start.4 = (f32[648,128]{1,0:T(8,128)S(1)}, f32[648,128]{1,0:T(8,128)S(1)}, u32[]{:S(2)}, u32[]{:S(2)}) collective-permute-start(f32[648,128]{1,0:T(8,128)S(1)} %get-tuple-element.20.refs_0_), channel_id=1, source_target_pairs={{0,4},{1,5},{2,6},{3,7},{4,0},{5,1},{6,2},{7,3},{8,12},{9,13},{10,... | collective-permute-start | bytes 995336 | tf_op jit(solution)/shard_map/ppermute | solution.py:239
  10.6 1.3 %collective-permute-start = (f32[648,128]{1,0:T(8,128)S(1)}, f32[648,128]{1,0:T(8,128)S(1)}, u32[]{:S(2)}, u32[]{:S(2)}) collective-permute-start(f32[648,128]{1,0:T(8,128)S(1)} %get-tuple-element.20.refs_0_), channel_id=1, source_target_pairs={{0,6},{1,7},{2,0},{3,1},{4,2},{5,3},{6,4},{7,5},{8,14},{9,15},{10,... | collective-permute-start | bytes 995336 | tf_op jit(solution)/shard_map/ppermute | solution.py:239
  12.0 5.3 %collective-permute-done.8.refs_0_ = f32[648,128]{1,0:T(8,128)S(1)} collective-permute-done((f32[648,128]{1,0:T(8,128)S(1)}, f32[648,128]{1,0:T(8,128)S(1)}, u32[]{:S(2)}, u32[]{:S(2)}) %collective-permute-start.8) | collective-permute-done | bytes 331808 | tf_op jit(solution)/shard_map/ppermute | solution.py:239
  17.3 1.8 %collective-permute-start.9 = (f32[648,128]{1,0:T(8,128)S(1)}, f32[648,128]{1,0:T(8,128)S(1)}, u32[]{:S(2)}, u32[]{:S(2)}) collective-permute-start(f32[648,128]{1,0:T(8,128)S(1)} %collective-permute-done.8.refs_0_), channel_id=1, source_target_pairs={{0,1},{1,0},{2,3},{3,2},{4,5},{5,4},{6,7},{7,6},{8,9},{9,8},{10,11... | collective-permute-start | bytes 995336 | tf_op jit(solution)/shard_map/ppermute | solution.py:236
  19.1 11.6 %collective-permute-done.4.refs_0_ = f32[648,128]{1,0:T(8,128)S(1)} collective-permute-done((f32[648,128]{1,0:T(8,128)S(1)}, f32[648,128]{1,0:T(8,128)S(1)}, u32[]{:S(2)}, u32[]{:S(2)}) %collective-permute-start.4) | collective-permute-done | bytes 331808 | tf_op jit(solution)/shard_map/ppermute | solution.py:239
  30.7 1.5 %collective-permute-start.5 = (f32[648,128]{1,0:T(8,128)S(1)}, f32[648,128]{1,0:T(8,128)S(1)}, u32[]{:S(2)}, u32[]{:S(2)}) collective-permute-start(f32[648,128]{1,0:T(8,128)S(1)} %collective-permute-done.4.refs_0_), channel_id=1, source_target_pairs={{0,1},{1,0},{2,3},{3,2},{4,5},{5,4},{6,7},{7,6},{8,9},{9,8},{10,11... | collective-permute-start | bytes 995336 | tf_op jit(solution)/shard_map/ppermute | solution.py:236
  34.2 4.5 %prep.1 = (bf16[1024,1024]{1,0:T(8,128)(2,1)S(1)}, bf16[1024,1024]{1,0:T(8,128)(2,1)}, f32[8,1024]{1,0:T(8,128)S(1)}, f32[256,1024]{1,0:T(8,128)S(1)}) custom-call(f32[1024,1024]{1,0:T(8,128)} %feat_ref.1, f32[1024,256]{1,0:T(8,128)S(1)} %copy-done.8), custom_call_target="tpu_custom_call" | custom-call | flops 4194304 | bytes 10485760 | tf_op jit(solution)/shard_map/prep/pallas_call | solution.py:98
  38.7 1.3 %copy-done.12 = bf16[1024,1024]{1,0:T(8,128)(2,1)} copy-done((bf16[1024,1024]{1,0:T(8,128)(2,1)}, bf16[1024,1024]{1,0:T(8,128)(2,1)S(1)}, u32[]{:S(2)}) %copy-start.12) | copy-done | bytes 2097176
  41.4 6.3 %plane.4 = (bf16[256,1024]{1,0:T(8,128)(2,1)S(1)}, bf16[256,1024]{1,0:T(8,128)(2,1)S(1)}, f32[256,1024]{1,0:T(8,128)S(1)}) custom-call(f32[648,128]{1,0:T(8,128)S(1)} %get-tuple-element.20.refs_0_, f32[648,128]{1,0:T(8,128)S(1)} %collective-permute-done.12.refs_1_, f32[648,128]{1,0:T(8,128)S(1)} %get-tuple-element.24.refs_2_, ...), custom_call_target="tpu_custom_call" | custom-call | flops 2013265920 | bytes 10485760 | tf_op jit(solution)/shard_map/plane/pallas_call | solution.py:170
  48.3 6.3 %plane.5 = (bf16[256,1024]{1,0:T(8,128)(2,1)S(1)}, bf16[256,1024]{1,0:T(8,128)(2,1)S(1)}, f32[256,1024]{1,0:T(8,128)S(1)}) custom-call(f32[648,128]{1,0:T(8,128)S(1)} %collective-permute-done.8.refs_0_, f32[648,128]{1,0:T(8,128)S(1)} %collective-permute-done.9.refs_1_, f32[648,128]{1,0:T(8,128)S(1)} %collective-permute-done.10.refs_2_, ...), custom_call_target="tpu_custom_call" | custom-call | flops 2013265920 | bytes 10485760 | tf_op jit(solution)/shard_map/plane/pallas_call | solution.py:170
  54.6 6.3 %plane.6 = (bf16[256,1024]{1,0:T(8,128)(2,1)S(1)}, bf16[256,1024]{1,0:T(8,128)(2,1)S(1)}, f32[256,1024]{1,0:T(8,128)S(1)}) custom-call(f32[648,128]{1,0:T(8,128)S(1)} %collective-permute-done.4.refs_0_, f32[648,128]{1,0:T(8,128)S(1)} %collective-permute-done.5.refs_1_, f32[648,128]{1,0:T(8,128)S(1)} %collective-permute-done.6.refs_2_, ...), custom_call_target="tpu_custom_call" | custom-call | flops 2013265920 | bytes 10485760 | tf_op jit(solution)/shard_map/plane/pallas_call | solution.py:170
  60.9 6.6 %plane.7 = (bf16[256,1024]{1,0:T(8,128)(2,1)S(1)}, bf16[256,1024]{1,0:T(8,128)(2,1)S(1)}, f32[256,1024]{1,0:T(8,128)S(1)}) custom-call(f32[648,128]{1,0:T(8,128)S(1)} %collective-permute-done.refs_0_, f32[648,128]{1,0:T(8,128)S(1)} %collective-permute-done.1.refs_1_, f32[648,128]{1,0:T(8,128)S(1)} %collective-permute-done.2.refs_2_, ...), custom_call_target="tpu_custom_call" | custom-call | flops 2013265920 | bytes 10485760 | tf_op jit(solution)/shard_map/plane/pallas_call | solution.py:170
  67.6 2.9 %grad.2 = f32[4,128,256]{2,1,0:T(8,128)} custom-call(f32[256,1024]{1,0:T(8,128)S(1)} %get-tuple-element.29.acc_ref, bf16[256,1024]{1,0:T(8,128)(2,1)S(1)} %get-tuple-element.30.refs_0_, bf16[256,1024]{1,0:T(8,128)(2,1)S(1)} %get-tuple-element.31.refs_1_, bf16[256,1024]{1,0:T(8,128)(2,1)S(1)} %get-tuple-element.32.refs_2_, ...), custom_call_target="tpu_custom_call" | custom-call | flops 805306368 | bytes 3145728 | tf_op jit(solution)/shard_map/grad/pallas_call | solution.py:208
  75.1 2.1 %grad.3 = f32[4,128,256]{2,1,0:T(8,128)S(1)} custom-call(f32[256,1024]{1,0:T(8,128)S(1)} %get-tuple-element.29.acc_ref, bf16[256,1024]{1,0:T(8,128)(2,1)S(1)} %get-tuple-element.30.refs_0_, bf16[256,1024]{1,0:T(8,128)(2,1)S(1)} %get-tuple-element.31.refs_1_, bf16[256,1024]{1,0:T(8,128)(2,1)S(1)} %copy-done.1, bf16[256,1024]{1,0:T(8,128)(2,1)S(1)} %copy-done.5, ...), custom_call_target="tpu_custom_call" | custom-call | flops 805306368 | bytes 3145728 | tf_op jit(solution)/shard_map/grad/pallas_call | solution.py:208
  78.4 1.5 %collective-permute-start.16 = (f32[4,32,256]{2,1,0:T(8,128)S(1)}, f32[4,32,256]{2,1,0:T(8,128)S(1)}, u32[]{:S(2)}, u32[]{:S(2)}) collective-permute-start(f32[4,32,256]{2,1,0:T(8,128)S(1)} %dynamic-slice_bitcast_fusion.1), channel_id=1, source_target_pairs={{0,16},{1,17},{2,18},{3,19},{4,20},{5,21},{6,22},{7,23},{8,24},{9,... | collective-permute-start | bytes 393224 | tf_op jit(solution)/shard_map/ppermute | solution.py:274
  80.0 1.6 %collective-permute-start.15 = (f32[4,32,256]{2,1,0:T(8,128)S(1)}, f32[4,32,256]{2,1,0:T(8,128)S(1)}, u32[]{:S(2)}, u32[]{:S(2)}) collective-permute-start(f32[4,32,256]{2,1,0:T(8,128)S(1)} %get-tuple-element.42), channel_id=1, source_target_pairs={{0,1},{1,0},{2,3},{3,2},{4,5},{5,4},{6,7},{7,6},{8,9},{9,8},{10,11... | collective-permute-start | bytes 393224 | tf_op jit(solution)/shard_map/ppermute | solution.py:274
  82.1 2.2 %collective-permute-done.16 = f32[4,32,256]{2,1,0:T(8,128)S(1)} collective-permute-done((f32[4,32,256]{2,1,0:T(8,128)S(1)}, f32[4,32,256]{2,1,0:T(8,128)S(1)}, u32[]{:S(2)}, u32[]{:S(2)}) %collective-permute-start.16) | collective-permute-done | bytes 131104 | tf_op jit(solution)/shard_map/ppermute | solution.py:274
  84.2 3.8 %collective-permute-done.15 = f32[4,32,256]{2,1,0:T(8,128)S(1)} collective-permute-done((f32[4,32,256]{2,1,0:T(8,128)S(1)}, f32[4,32,256]{2,1,0:T(8,128)S(1)}, u32[]{:S(2)}, u32[]{:S(2)}) %collective-permute-start.15) | collective-permute-done | bytes 131104 | tf_op jit(solution)/shard_map/ppermute | solution.py:274
  88.1 8.7 %collective-permute-start.18 = (f32[32,256]{1,0:T(8,128)S(1)}, f32[32,256]{1,0:T(8,128)S(1)}, u32[]{:S(2)}, u32[]{:S(2)}) collective-permute-start(f32[32,256]{1,0:T(8,128)S(1)} %get-tuple-element.44), channel_id=1, source_target_pairs={{0,6},{1,7},{2,0},{3,1},{4,2},{5,3},{6,4},{7,5},{8,14},{9,15},{10,... | collective-permute-start | bytes 98312 | tf_op jit(solution)/shard_map/ppermute | solution.py:239
  97.3 1.9 %collective-permute-start.20 = (f32[32,256]{1,0:T(8,128)S(1)}, f32[32,256]{1,0:T(8,128)S(1)}, u32[]{:S(2)}, u32[]{:S(2)}) collective-permute-start(f32[32,256]{1,0:T(8,128)S(1)} %get-tuple-element.45), channel_id=1, source_target_pairs={{0,2},{1,3},{2,4},{3,5},{4,6},{5,7},{6,0},{7,1},{8,10},{9,11},{10,... | collective-permute-start | bytes 98312 | tf_op jit(solution)/shard_map/ppermute | solution.py:239
  101.7 1.4 %collective-permute-done.20 = f32[32,256]{1,0:T(8,128)S(1)} collective-permute-done((f32[32,256]{1,0:T(8,128)S(1)}, f32[32,256]{1,0:T(8,128)S(1)}, u32[]{:S(2)}, u32[]{:S(2)}) %collective-permute-start.20) | collective-permute-done | bytes 32800 | tf_op jit(solution)/shard_map/ppermute | solution.py:239
  103.0 5.4 %all_gather.3 = f32[128,256]{1,0:T(8,128)S(1)} all-gather(f32[32,256]{1,0:T(8,128)S(1)} %fusion.5), channel_id=1, replica_groups=mesh['grp'=4,'own'=8] {'grp'}, dimensions={0}, use_global_device_ids=true | all-gather | bytes 163840 | tf_op jit(solution)/shard_map/all_gather | solution.py:280
  (62 shorter events, 16.7 us)
Async XLA Ops:
  3.5 13.8 %collective-permute-start.8 = (f32[648,128]{1,0:T(8,128)S(1)}, f32[648,128]{1,0:T(8,128)S(1)}, u32[]{:S(2)}, u32[]{:S(2)}) collective-permute-start(f32[648,128]{1,0:T(8,128)S(1)} %get-tuple-element.20.refs_0_), channel_id=1, source_target_pairs={{0,2},{1,3},{2,4},{3,5},{4,6},{5,7},{6,0},{7,1},{8,10},{9,11},{10,... | collective-permute-start | bytes 995336 | tf_op jit(solution)/shard_map/ppermute | solution.py:239
  6.5 12.6 %collective-permute-start.12 = (f32[648,128]{1,0:T(8,128)S(1)}, f32[648,128]{1,0:T(8,128)S(1)}, u32[]{:S(2)}, u32[]{:S(2)}) collective-permute-start(f32[648,128]{1,0:T(8,128)S(1)} %get-tuple-element.20.refs_0_), channel_id=1, source_target_pairs={{0,1},{1,0},{2,3},{3,2},{4,5},{5,4},{6,7},{7,6},{8,9},{9,8},{10,11... | collective-permute-start | bytes 995336 | tf_op jit(solution)/shard_map/ppermute | solution.py:236
  8.0 22.7 %collective-permute-start.4 = (f32[648,128]{1,0:T(8,128)S(1)}, f32[648,128]{1,0:T(8,128)S(1)}, u32[]{:S(2)}, u32[]{:S(2)}) collective-permute-start(f32[648,128]{1,0:T(8,128)S(1)} %get-tuple-element.20.refs_0_), channel_id=1, source_target_pairs={{0,4},{1,5},{2,6},{3,7},{4,0},{5,1},{6,2},{7,3},{8,12},{9,13},{10,... | collective-permute-start | bytes 995336 | tf_op jit(solution)/shard_map/ppermute | solution.py:239
  10.6 21.6 %collective-permute-start = (f32[648,128]{1,0:T(8,128)S(1)}, f32[648,128]{1,0:T(8,128)S(1)}, u32[]{:S(2)}, u32[]{:S(2)}) collective-permute-start(f32[648,128]{1,0:T(8,128)S(1)} %get-tuple-element.20.refs_0_), channel_id=1, source_target_pairs={{0,6},{1,7},{2,0},{3,1},{4,2},{5,3},{6,4},{7,5},{8,14},{9,15},{10,... | collective-permute-start | bytes 995336 | tf_op jit(solution)/shard_map/ppermute | solution.py:239
  17.3 15.4 %collective-permute-start.9 = (f32[648,128]{1,0:T(8,128)S(1)}, f32[648,128]{1,0:T(8,128)S(1)}, u32[]{:S(2)}, u32[]{:S(2)}) collective-permute-start(f32[648,128]{1,0:T(8,128)S(1)} %collective-permute-done.8.refs_0_), channel_id=1, source_target_pairs={{0,1},{1,0},{2,3},{3,2},{4,5},{5,4},{6,7},{7,6},{8,9},{9,8},{10,11... | collective-permute-start | bytes 995336 | tf_op jit(solution)/shard_map/ppermute | solution.py:236
  19.1 21.0 %collective-permute-start.13 = (f32[648,128]{1,0:T(8,128)S(1)}, f32[648,128]{1,0:T(8,128)S(1)}, u32[]{:S(2)}, u32[]{:S(2)}) collective-permute-start(f32[648,128]{1,0:T(8,128)S(1)} %collective-permute-done.12.refs_1_), channel_id=1, source_target_pairs={{0,8},{8,0},{16,24},{24,16},{1,9},{9,1},{17,25},{25,17},{2,10},{10... | collective-permute-start | bytes 995336 | tf_op jit(solution)/shard_map/ppermute | solution.py:233
  30.7 10.7 %collective-permute-start.5 = (f32[648,128]{1,0:T(8,128)S(1)}, f32[648,128]{1,0:T(8,128)S(1)}, u32[]{:S(2)}, u32[]{:S(2)}) collective-permute-start(f32[648,128]{1,0:T(8,128)S(1)} %collective-permute-done.4.refs_0_), channel_id=1, source_target_pairs={{0,1},{1,0},{2,3},{3,2},{4,5},{5,4},{6,7},{7,6},{8,9},{9,8},{10,11... | collective-permute-start | bytes 995336 | tf_op jit(solution)/shard_map/ppermute | solution.py:236
  32.2 15.4 %collective-permute-start.10 = (f32[648,128]{1,0:T(8,128)S(1)}, f32[648,128]{1,0:T(8,128)S(1)}, u32[]{:S(2)}, u32[]{:S(2)}) collective-permute-start(f32[648,128]{1,0:T(8,128)S(1)} %collective-permute-done.8.refs_0_), channel_id=1, source_target_pairs={{0,8},{8,0},{16,24},{24,16},{1,9},{9,1},{17,25},{25,17},{2,10},{10... | collective-permute-start | bytes 995336 | tf_op jit(solution)/shard_map/ppermute | solution.py:233
  32.2 16.0 %collective-permute-start.1 = (f32[648,128]{1,0:T(8,128)S(1)}, f32[648,128]{1,0:T(8,128)S(1)}, u32[]{:S(2)}, u32[]{:S(2)}) collective-permute-start(f32[648,128]{1,0:T(8,128)S(1)} %collective-permute-done.refs_0_), channel_id=1, source_target_pairs={{0,1},{1,0},{2,3},{3,2},{4,5},{5,4},{6,7},{7,6},{8,9},{9,8},{10,11... | collective-permute-start | bytes 995336 | tf_op jit(solution)/shard_map/ppermute | solution.py:236
  32.7 15.6 %collective-permute-start.11 = (f32[648,128]{1,0:T(8,128)S(1)}, f32[648,128]{1,0:T(8,128)S(1)}, u32[]{:S(2)}, u32[]{:S(2)}) collective-permute-start(f32[648,128]{1,0:T(8,128)S(1)} %collective-permute-done.9.refs_1_), channel_id=1, source_target_pairs={{0,8},{8,0},{16,24},{24,16},{1,9},{9,1},{17,25},{25,17},{2,10},{10... | collective-permute-start | bytes 995336 | tf_op jit(solution)/shard_map/ppermute | solution.py:233
  40.0 14.6 %collective-permute-start.6 = (f32[648,128]{1,0:T(8,128)S(1)}, f32[648,128]{1,0:T(8,128)S(1)}, u32[]{:S(2)}, u32[]{:S(2)}) collective-permute-start(f32[648,128]{1,0:T(8,128)S(1)} %collective-permute-done.4.refs_0_), channel_id=1, source_target_pairs={{0,8},{8,0},{16,24},{24,16},{1,9},{9,1},{17,25},{25,17},{2,10},{10... | collective-permute-start | bytes 995336 | tf_op jit(solution)/shard_map/ppermute | solution.py:233
  41.4 13.2 %collective-permute-start.7 = (f32[648,128]{1,0:T(8,128)S(1)}, f32[648,128]{1,0:T(8,128)S(1)}, u32[]{:S(2)}, u32[]{:S(2)}) collective-permute-start(f32[648,128]{1,0:T(8,128)S(1)} %collective-permute-done.5.refs_1_), channel_id=1, source_target_pairs={{0,8},{8,0},{16,24},{24,16},{1,9},{9,1},{17,25},{25,17},{2,10},{10... | collective-permute-start | bytes 995336 | tf_op jit(solution)/shard_map/ppermute | solution.py:233
  47.7 13.3 %collective-permute-start.2 = (f32[648,128]{1,0:T(8,128)S(1)}, f32[648,128]{1,0:T(8,128)S(1)}, u32[]{:S(2)}, u32[]{:S(2)}) collective-permute-start(f32[648,128]{1,0:T(8,128)S(1)} %collective-permute-done.refs_0_), channel_id=1, source_target_pairs={{0,8},{8,0},{16,24},{24,16},{1,9},{9,1},{17,25},{25,17},{2,10},{10... | collective-permute-start | bytes 995336 | tf_op jit(solution)/shard_map/ppermute | solution.py:233
  48.2 12.7 %collective-permute-start.3 = (f32[648,128]{1,0:T(8,128)S(1)}, f32[648,128]{1,0:T(8,128)S(1)}, u32[]{:S(2)}, u32[]{:S(2)}) collective-permute-start(f32[648,128]{1,0:T(8,128)S(1)} %collective-permute-done.1.refs_1_), channel_id=1, source_target_pairs={{0,8},{8,0},{16,24},{24,16},{1,9},{9,1},{17,25},{25,17},{2,10},{10... | collective-permute-start | bytes 995336 | tf_op jit(solution)/shard_map/ppermute | solution.py:233
  60.9 6.7 %copy-start = (bf16[256,1024]{1,0:T(8,128)(2,1)}, bf16[256,1024]{1,0:T(8,128)(2,1)S(1)}, u32[]{:S(2)}) copy-start(bf16[256,1024]{1,0:T(8,128)(2,1)S(1)} %get-tuple-element.32.refs_2_) | copy-start | bytes 1572868
  60.9 6.7 %copy-start.2 = (bf16[256,1024]{1,0:T(8,128)(2,1)}, bf16[256,1024]{1,0:T(8,128)(2,1)S(1)}, u32[]{:S(2)}) copy-start(bf16[256,1024]{1,0:T(8,128)(2,1)S(1)} %get-tuple-element.36.refs_6_) | copy-start | bytes 1572868
  67.5 3.0 %copy-start.4 = (bf16[256,1024]{1,0:T(8,128)(2,1)}, bf16[256,1024]{1,0:T(8,128)(2,1)S(1)}, u32[]{:S(2)}) copy-start(bf16[256,1024]{1,0:T(8,128)(2,1)S(1)} %get-tuple-element.33.refs_3_) | copy-start | bytes 1572868
  70.5 6.7 %collective-permute-start.14 = (f32[4,128,256]{2,1,0:T(8,128)}, f32[4,128,256]{2,1,0:T(8,128)}, u32[]{:S(2)}, u32[]{:S(2)}) collective-permute-start(f32[4,128,256]{2,1,0:T(8,128)} %grad.2), channel_id=1, source_target_pairs={{0,8},{8,0},{16,24},{24,16},{1,9},{9,1},{17,25},{25,17},{2,10},{10... | collective-permute-start | bytes 1572872 | tf_op jit(solution)/shard_map/ppermute | solution.py:233
  78.4 5.8 %collective-permute-start.16 = (f32[4,32,256]{2,1,0:T(8,128)S(1)}, f32[4,32,256]{2,1,0:T(8,128)S(1)}, u32[]{:S(2)}, u32[]{:S(2)}) collective-permute-start(f32[4,32,256]{2,1,0:T(8,128)S(1)} %dynamic-slice_bitcast_fusion.1), channel_id=1, source_target_pairs={{0,16},{1,17},{2,18},{3,19},{4,20},{5,21},{6,22},{7,23},{8,24},{9,... | collective-permute-start | bytes 393224 | tf_op jit(solution)/shard_map/ppermute | solution.py:274
  80.0 8.1 %collective-permute-start.15 = (f32[4,32,256]{2,1,0:T(8,128)S(1)}, f32[4,32,256]{2,1,0:T(8,128)S(1)}, u32[]{:S(2)}, u32[]{:S(2)}) collective-permute-start(f32[4,32,256]{2,1,0:T(8,128)S(1)} %get-tuple-element.42), channel_id=1, source_target_pairs={{0,1},{1,0},{2,3},{3,2},{4,5},{5,4},{6,7},{7,6},{8,9},{9,8},{10,11... | collective-permute-start | bytes 393224 | tf_op jit(solution)/shard_map/ppermute | solution.py:274
  81.6 6.5 %collective-permute-start.17 = (f32[4,32,256]{2,1,0:T(8,128)S(1)}, f32[4,32,256]{2,1,0:T(8,128)S(1)}, u32[]{:S(2)}, u32[]{:S(2)}) collective-permute-start(f32[4,32,256]{2,1,0:T(8,128)S(1)} %get-tuple-element.43), channel_id=1, source_target_pairs={{0,17},{1,16},{2,19},{3,18},{4,21},{5,20},{6,23},{7,22},{8,25},{9,... | collective-permute-start | bytes 393224 | tf_op jit(solution)/shard_map/ppermute | solution.py:274
  88.1 12.4 %collective-permute-start.18 = (f32[32,256]{1,0:T(8,128)S(1)}, f32[32,256]{1,0:T(8,128)S(1)}, u32[]{:S(2)}, u32[]{:S(2)}) collective-permute-start(f32[32,256]{1,0:T(8,128)S(1)} %get-tuple-element.44), channel_id=1, source_target_pairs={{0,6},{1,7},{2,0},{3,1},{4,2},{5,3},{6,4},{7,5},{8,14},{9,15},{10,... | collective-permute-start | bytes 98312 | tf_op jit(solution)/shard_map/ppermute | solution.py:239
  96.9 4.8 %collective-permute-start.19 = (f32[32,256]{1,0:T(8,128)S(1)}, f32[32,256]{1,0:T(8,128)S(1)}, u32[]{:S(2)}, u32[]{:S(2)}) collective-permute-start(f32[32,256]{1,0:T(8,128)S(1)} %get-tuple-element.46), channel_id=1, source_target_pairs={{0,4},{1,5},{2,6},{3,7},{4,0},{5,1},{6,2},{7,3},{8,12},{9,13},{10,... | collective-permute-start | bytes 98312 | tf_op jit(solution)/shard_map/ppermute | solution.py:239
  97.3 5.7 %collective-permute-start.20 = (f32[32,256]{1,0:T(8,128)S(1)}, f32[32,256]{1,0:T(8,128)S(1)}, u32[]{:S(2)}, u32[]{:S(2)}) collective-permute-start(f32[32,256]{1,0:T(8,128)S(1)} %get-tuple-element.45), channel_id=1, source_target_pairs={{0,2},{1,3},{2,4},{3,5},{4,6},{5,7},{6,0},{7,1},{8,10},{9,11},{10,... | collective-permute-start | bytes 98312 | tf_op jit(solution)/shard_map/ppermute | solution.py:239
  (10 other events, 12.3 us)

commit v2 on v1

v2 whole, which is shorter than its diff:
```python
import functools

import jax
import jax.numpy as jnp
from jax import lax
from jax.experimental import pallas as pl
from jax.experimental.pallas import tpu as pltpu
from jax.sharding import PartitionSpec as P

LANES = 128
F32 = jnp.float32
BF16 = jnp.bfloat16
NT = (((1,), (1,)), ((), ()))
NN = (((1,), (0,)), ((), ()))


VMEM = pl.BlockSpec(memory_space=pltpu.VMEM)
SMEM = pl.BlockSpec(memory_space=pltpu.SMEM)


def params(mib=16):
    return pltpu.CompilerParams(vmem_limit_bytes=mib * 1024 * 1024)


def split(value):
    high = value.astype(BF16)
    return high, (value - high.astype(F32)).astype(BF16)


def mm(a, b, dims):
    return lax.dot_general(a, b, dims, preferred_element_type=F32)


def pack_kernel(parts, place_ref, cen_ref, coef_ref, width_ref, mine_ref, sib_ref, col_ref):
    count, depth = cen_ref.shape
    piece = count // (2 * parts)
    blocks = depth // LANES
    size = mine_ref.shape[0] // parts
    col_ref[...] = jnp.transpose(jnp.broadcast_to(1.0 / width_ref[...], (count, count)))
    cols, squares = [], []
    for which, out in enumerate((mine_ref, sib_ref)):
        core = place_ref[1] if which == 0 else 1 - place_ref[1]
        for ahead in range(parts):
            part = lax.rem(place_ref[0] + ahead, parts)
            rows = pl.ds(pl.multiple_of((part * 2 + core) * piece, piece), piece)
            total = jnp.zeros((piece, LANES), F32)
            at = ahead * size
            for block in range(blocks):
                value = cen_ref[rows, block * LANES:(block + 1) * LANES]
                out[at:at + piece, :] = value
                total = total + value * value
                at += piece
            for block in range(coef_ref.shape[1] // LANES):
                out[at:at + piece, :] = coef_ref[rows, block * LANES:(block + 1) * LANES]
                at += piece
            cols.append(col_ref[rows, :])
            squares.append(total)
    inverse = jnp.transpose(jnp.concatenate(cols, axis=0))[:1]
    square = 0.5 * jnp.sum(jnp.transpose(jnp.concatenate(squares, axis=0)), axis=0, keepdims=True)
    for which, out in enumerate((mine_ref, sib_ref)):
        for ahead in range(parts):
            tail = jnp.concatenate([inverse, square] + [jnp.zeros((6, LANES), F32)], axis=0)
            out[(ahead + 1) * size - 8:(ahead + 1) * size, :] = tail
            inverse = jnp.concatenate([inverse[:, piece:], inverse[:, :piece]], axis=1)
            square = jnp.concatenate([square[:, piece:], square[:, :piece]], axis=1)


def pack(place, centres, coefficients, widths, parts):
    count, depth = centres.shape
    width = coefficients.shape[1]
    rows = count // 2 * ((depth + width) // LANES) + 8 * parts
    shape = jax.ShapeDtypeStruct((rows, LANES), F32)
    out = pl.BlockSpec((rows, LANES), lambda i: (0, 0))
    return pl.pallas_call(
        functools.partial(pack_kernel, parts),
        grid=(1,),
        out_shape=(shape, shape),
        in_specs=[
            SMEM,
            pl.BlockSpec((count, depth), lambda i: (0, 0)),
            pl.BlockSpec((count, width), lambda i: (0, 0)),
            pl.BlockSpec((1, count), lambda i: (0, 0)),
        ],
        out_specs=(out, out),
        scratch_shapes=[pltpu.VMEM((count, LANES), F32)],
        compiler_params=params(),
        name="pack",
    )(place, centres, coefficients, widths)


def prep_kernel(feat_ref, tgt_ref, high_ref, low_ref, sq_ref, acc_ref):
    value = feat_ref[...]
    high, low = split(value)
    high_ref[...] = high
    low_ref[...] = low
    square = value * value
    total = square[:, :LANES]
    for block in range(1, value.shape[1] // LANES):
        total = total + square[:, block * LANES:(block + 1) * LANES]
    row = 0.5 * jnp.sum(jnp.transpose(total), axis=0, keepdims=True)
    sq_ref[...] = jnp.broadcast_to(row, sq_ref.shape)
    acc_ref[...] = -jnp.transpose(tgt_ref[...])


def prep(features, targets, step):
    rows, depth = features.shape
    width = targets.shape[1]
    return pl.pallas_call(
        prep_kernel,
        grid=(rows // step,),
        out_shape=(
            jax.ShapeDtypeStruct((rows, depth), BF16),
            jax.ShapeDtypeStruct((rows, depth), BF16),
            jax.ShapeDtypeStruct((8, rows), F32),
            jax.ShapeDtypeStruct((width, rows), F32),
        ),
        in_specs=[pl.BlockSpec((step, depth), lambda i: (i, 0)), pl.BlockSpec((step, width), lambda i: (i, 0))],
        out_specs=(
            pl.BlockSpec((step, depth), lambda i: (i, 0)),
            pl.BlockSpec((step, depth), lambda i: (i, 0)),
            pl.BlockSpec((8, step), lambda i: (0, i)),
            pl.BlockSpec((width, step), lambda i: (0, i)),
        ),
        compiler_params=params(),
        cost_estimate=pl.CostEstimate(flops=4 * rows * depth, bytes_accessed=10 * rows * depth, transcendentals=0),
        name="prep",
    )(features, targets)


def plane_kernel(parts, number, piece, *refs):
    messages = refs[:number]
    fh_ref, fl_ref, sq_ref, acc_ref, kh_ref, kl_ref, out_ref, cen_ref, tmp_ref, coef_ref, inv_ref, cs_ref = refs[number:]
    depth, width, count = fh_ref.shape[1], acc_ref.shape[0], kh_ref.shape[0]
    size = piece * ((depth + width) // LANES) + 8
    at = 0
    for message in messages:
        for start in range(0, message.shape[0], size):
            for block in range(depth // LANES):
                high, low = split(message[start:start + piece, :])
                lanes = slice(block * LANES, (block + 1) * LANES)
                cen_ref[at:at + piece, lanes] = high
                cen_ref[count + at:count + at + piece, lanes] = low
                start += piece
            for block in range(width // LANES):
                tmp_ref[at:at + piece, block * LANES:(block + 1) * LANES] = message[start:start + piece, :]
                start += piece
            for row, into in ((0, inv_ref), (1, cs_ref)):
                line = jnp.broadcast_to(message[start + row:start + row + 1, :], (LANES, LANES))
                into[at:at + piece, :] = jnp.transpose(line)[:piece]
            at += piece
    high, low = split(jnp.transpose(tmp_ref[...]))
    coef_ref[:width, :] = high
    coef_ref[width:, :] = low
    both = mm(cen_ref[...], fh_ref[...], NT)
    cross = both[:count] + both[count:] + mm(cen_ref[:count, :], fl_ref[...], NT)
    wide = cross.shape[1] // LANES
    cs = jnp.concatenate([cs_ref[...]] * wide, axis=1)
    inv = jnp.concatenate([inv_ref[...]] * wide, axis=1)
    kh, kl = split(jnp.exp((cross - cs - sq_ref[:1, :]) * inv))
    kh_ref[...] = kh
    kl_ref[...] = kl
    both = mm(coef_ref[...], kh, NN)
    out_ref[...] = acc_ref[...] + (both[:width] + both[width:] + mm(coef_ref[:width, :], kl, NN))


def plane(messages, fh, fl, sq, acc, parts, piece):
    rows, depth = fh.shape
    width = acc.shape[0]
    count = 4 * parts * piece
    return pl.pallas_call(
        functools.partial(plane_kernel, parts, len(messages), piece),
        out_shape=(
            jax.ShapeDtypeStruct((count, rows), BF16),
            jax.ShapeDtypeStruct((count, rows), BF16),
            jax.ShapeDtypeStruct((width, rows), F32),
        ),
        in_specs=[VMEM] * (len(messages) + 4),
        out_specs=(VMEM, VMEM, VMEM),
        scratch_shapes=[
            pltpu.VMEM((2 * count, depth), BF16),
            pltpu.VMEM((count, width), F32),
            pltpu.VMEM((2 * width, count), BF16),
            pltpu.VMEM((count, LANES), F32),
            pltpu.VMEM((count, LANES), F32),
        ],
        compiler_params=params(),
        cost_estimate=pl.CostEstimate(
            flops=6 * rows * count * (depth + width), bytes_accessed=4 * rows * depth, transcendentals=rows * count
        ),
        name="plane",
    )(*messages, fh, fl, sq, acc)


def grad_kernel(planes, which, acc_ref, *refs):
    kh_refs, kl_refs, out_ref = refs[:planes], refs[planes:2 * planes], refs[2 * planes]
    count = out_ref.shape[1]
    high, low = split(acc_ref[...])
    for k in range(planes):
        kh = kh_refs[k][which * count:(which + 1) * count, :]
        kl = kl_refs[k][which * count:(which + 1) * count, :]
        both = mm(jnp.concatenate([kh, kl], axis=0), high, NT)
        out_ref[k] = both[:count] + both[count:] + mm(kh, low, NT)


def grad(acc, khs, kls, which):
    width, rows = acc.shape
    count = khs[0].shape[0] // 2
    planes = len(khs)
    return pl.pallas_call(
        functools.partial(grad_kernel, planes, which),
        out_shape=jax.ShapeDtypeStruct((planes, count, width), F32),
        in_specs=[VMEM] * (1 + 2 * planes),
        out_specs=VMEM,
        compiler_params=params(),
        cost_estimate=pl.CostEstimate(
            flops=6 * rows * count * width * planes, bytes_accessed=4 * rows * width, transcendentals=0
        ),
        name="grad",
    )(acc, *khs, *kls)


def halve_kernel(kept_ref, sent_ref, *outs):
    piece = outs[0].shape[1]
    for n, out in enumerate(outs):
        rows = slice(n * piece, (n + 1) * piece)
        out[...] = kept_ref[:, rows, :] + sent_ref[:, rows, :]


def halve(kept, sent, number):
    deep, count, width = kept.shape
    return pl.pallas_call(
        halve_kernel,
        out_shape=[jax.ShapeDtypeStruct((deep, count // number, width), F32)] * number,
        in_specs=[VMEM] * 2,
        out_specs=[VMEM] * number,
        compiler_params=params(),
        name="halve",
    )(kept, sent)


def join_kernel(parts, place_ref, *refs):
    pieces, out_ref = refs[:-1], refs[-1]
    piece = pieces[0].shape[0]
    for ahead in range(parts):
        for other in range(2):
            part = lax.rem(place_ref[0] + ahead, parts)
            core = place_ref[1] if other == 0 else 1 - place_ref[1]
            rows = pl.ds(pl.multiple_of((part * 2 + core) * piece, piece), piece)
            out_ref[rows, :] = pieces[ahead * 2 + other][...]


def join(place, pieces, parts):
    piece, width = pieces[0].shape
    return pl.pallas_call(
        functools.partial(join_kernel, parts),
        out_shape=jax.ShapeDtypeStruct((piece * len(pieces), width), F32),
        in_specs=[SMEM] + [VMEM] * len(pieces),
        out_specs=VMEM,
        compiler_params=params(),
        name="join",
    )(place, *pieces)


def after(value, *tokens):
    return lax.optimization_barrier((value,) + tokens)[0]


def body(groups, owners, features, targets, centres, widths, coefficients):
    rows, depth = features.shape
    width = targets.shape[1]
    count = centres.shape[0]
    parts = groups // 2
    piece = count // groups
    deep = owners // 2
    me = lax.axis_index("grp")
    place = jnp.stack([me // 2, me % 2])

    def move(value, ahead=0, core=0, k=0, y=0):
        pairs = []
        for g in range(groups):
            for o in range(owners):
                to = ((g // 2 + ahead) % parts) * 2 + (g % 2 + core) % 2
                pairs.append((g * owners + o, to * owners + ((o // 2 + k) % deep) * 2 + (o + y) % 2))
        return lax.ppermute(value, ("grp", "own"), pairs)

    mine, sib = pack(place, centres, coefficients, widths.reshape(1, count), parts)
    order = sorted(range(1, deep), key=lambda k: min(k, deep - k))
    near = move(mine, y=1)
    far = {k: move(mine, k=k) for k in order}
    fh, fl, sq, acc = prep(features, targets, min(rows, 256))
    messages = (mine, near, sib, move(near, core=1))
    khs, kls = {}, {}
    khs[0], kls[0], acc = plane(messages, fh, fl, sq, acc, parts, piece)
    accs = [sq, sq, acc]
    others = {}
    for n, k in enumerate(order):
        same = after(far[k], accs[n]) if n < 3 else far[k]
        far[k] = same
        others[k] = move(same, y=1)
    for n, k in enumerate(order):
        same, other = far[k], others[k]
        if n == len(order) - 1:
            other = after(other, acc)
        messages = (same, other, move(same, core=1), move(other, core=1))
        khs[k], kls[k], acc = plane(messages, fh, fl, sq, acc, parts, piece)
    khs = [khs[k] for k in range(deep)]
    kls = [kls[k] for k in range(deep)]

    sent = move(grad(acc, khs, kls, 1), core=1)
    kept = grad(acc, khs, kls, 0)
    residual = jnp.transpose(acc)
    pieces = halve(kept, sent, 2 * parts)
    owned = pieces[0]
    for other in range(2):
        for ahead in range(parts):
            if ahead or other:
                owned = owned + move(pieces[other * parts + ahead], ahead=ahead, y=other)
    factor = 1.0 / jnp.sqrt(F32(rows * groups * owners))
    gradient = owned[0]
    for k in range(1, deep):
        gradient = gradient + move(owned[k], k=-k)
    gradient = gradient * factor
    pieces = []
    for ahead in range(parts):
        for core in range(2):
            pieces.append(move(gradient, ahead=-ahead, core=core) if ahead or core else gradient)
    return residual, join(place, pieces, parts)


def solution(mesh):
    return jax.shard_map(
        functools.partial(body, mesh.shape["grp"], mesh.shape["own"]),
        mesh=mesh,
        in_specs=(
            P(("grp", "own"), None),
            P(("grp", "own"), None),
            P("own", None),
            P("own"),
            P("own", None),
        ),
        out_specs=(P(("grp", "own"), None), P("own", None)),
        check_vma=False,
    )
```

time: 110 us -> 85 us (0.77)
  Pallas kernels: 35.2 us -> 16 us
  waiting for transfers between devices: 26.5 us -> 38.2 us
  starting transfers between devices: 28.7 us -> 22.3 us
  blocking collectives: 5.43 us -> 0 us
  local copies, waits for them, and re-layouts: 11.4 us -> 7.33 us
    pallas_call x7 -> x9, Pallas kernels: 30.7 us -> 14.5 us  [the longest x4 9.6 us: plane(): pl.pallas_call(functools.partial(plane_kernel, parts, len(messages), piec...]
    ppermute x21 -> x24, waiting for transfers between devices: 26.5 us -> 38.2 us  [move(): return lax.ppermute(value, ('grp', 'own'), pairs)]
    ppermute x21 -> x24, starting transfers between devices: 28.7 us -> 22.3 us  [move(): return lax.ppermute(value, ('grp', 'own'), pairs)]
    all_gather x1 -> x0, blocking collectives: 5.43 us -> none  [body(): gradient = lax.all_gather(gradient * factor, 'grp', axis=0, tiled=True)]
    unnamed x28 -> x11, local copies, waits for them, and re-layouts: 11.3 us -> 7.32 us
    pallas_call x1, Pallas kernels: 4.51 us -> 1.45 us  [prep(): pl.pallas_call(prep_kernel, grid=(rows // step,), out_shape=(jax.ShapeDty...]
    add x2 -> x1, other arithmetic: 1.15 us -> 0.04 us  [body(): owned = owned + move(pieces[other * parts + ahead], ahead=ahead, y=other)]
  transfers between devices with their start and end apart: 21 -> 24, of which waited for: 7 -> 13; matrix products, arithmetic and copies ran while one was open for 1% -> 2% of each run, Pallas kernels for 23% -> 12%
where the time goes in v2:
time: 85 us; the launch traced here: 84.7 us
  waiting for transfers between devices  38.2 us (45%)
  starting transfers between devices  22.3 us (26%)
  Pallas kernels  16 us (19%)
  local copies, waits for them, and re-layouts  7.33 us (9%)
    ppermute x24, waiting for transfers between devices, move(): return lax.ppermute(value, ('grp', 'own'), pairs)  38.2 us
    ppermute x24, starting transfers between devices, move(): return lax.ppermute(value, ('grp', 'own'), pairs)  22.3 us
    pallas_call x4, Pallas kernels, plane(): pl.pallas_call(functools.partial(plane_kernel, parts, len(messages), piec...  9.6 us
    unnamed x11, local copies, waits for them, and re-layouts  7.32 us
    pallas_call x2, Pallas kernels, grad(): pl.pallas_call(functools.partial(grad_kernel, planes, which), out_shape=j...  2.72 us
  transfers between devices with their start and end apart: 24, of which 13 were waited for; matrix products, arithmetic and copies ran while one was open for 2% of the time, Pallas kernels for 12%

profile of v2, /device:TPU:0, one launch (start us, length us, event | category | flops | bytes accessed | tf_op | source)
XLA Modules:
  0.0 84.7 jit_solution(8809435541841079658)
XLA Ops:
  4.2 3.0 %collective-permute-start.8 = (f32[656,128]{1,0:T(8,128)S(1)}, f32[656,128]{1,0:T(8,128)S(1)}, u32[]{:S(2)}, u32[]{:S(2)}) collective-permute-start(f32[656,128]{1,0:T(8,128)S(1)} %get-tuple-element.28.refs_0_), channel_id=1, source_target_pairs={{0,2},{1,3},{2,4},{3,5},{4,6},{5,7},{6,0},{7,1},{8,10},{9,11},{10,... | collective-permute-start | bytes 1007624 | tf_op jit(solution)/shard_map/ppermute | solution.py:284
  7.3 2.0 %collective-permute-start.4 = (f32[656,128]{1,0:T(8,128)S(1)}, f32[656,128]{1,0:T(8,128)S(1)}, u32[]{:S(2)}, u32[]{:S(2)}) collective-permute-start(f32[656,128]{1,0:T(8,128)S(1)} %get-tuple-element.28.refs_0_), channel_id=1, source_target_pairs={{0,6},{1,7},{2,0},{3,1},{4,2},{5,3},{6,4},{7,5},{8,14},{9,15},{10,... | collective-permute-start | bytes 1007624 | tf_op jit(solution)/shard_map/ppermute | solution.py:284
  9.3 1.7 %collective-permute-start.1 = (f32[656,128]{1,0:T(8,128)S(1)}, f32[656,128]{1,0:T(8,128)S(1)}, u32[]{:S(2)}, u32[]{:S(2)}) collective-permute-start(f32[656,128]{1,0:T(8,128)S(1)} %get-tuple-element.28.refs_0_), channel_id=1, source_target_pairs={{0,1},{1,0},{2,3},{3,2},{4,5},{5,4},{6,7},{7,6},{8,9},{9,8},{10,11... | collective-permute-start | bytes 1007624 | tf_op jit(solution)/shard_map/ppermute | solution.py:284
  11.0 2.2 %copy-done = f32[1024,1024]{1,0:T(8,128)S(1)} copy-done((f32[1024,1024]{1,0:T(8,128)S(1)}, f32[1024,1024]{1,0:T(8,128)}, u32[]{:S(2)}) %copy-start) | copy-done | bytes 4194328
  14.5 1.5 %prep.1 = (bf16[1024,1024]{1,0:T(8,128)(2,1)S(1)}, bf16[1024,1024]{1,0:T(8,128)(2,1)S(1)}, f32[8,1024]{1,0:T(8,128)S(1)}, f32[256,1024]{1,0:T(8,128)S(1)}) custom-call(f32[1024,1024]{1,0:T(8,128)S(1)} %copy-done, f32[1024,256]{1,0:T(8,128)S(1)} %copy-done.1), custom_call_target="tpu_custom_call" | custom-call | flops 4194304 | bytes 10485760 | tf_op jit(solution)/shard_map/prep/pallas_call | solution.py:108
  15.9 2.1 %collective-permute-done.8.refs_0_ = f32[656,128]{1,0:T(8,128)S(1)} collective-permute-done((f32[656,128]{1,0:T(8,128)S(1)}, f32[656,128]{1,0:T(8,128)S(1)}, u32[]{:S(2)}, u32[]{:S(2)}) %collective-permute-start.8) | collective-permute-done | bytes 335904 | tf_op jit(solution)/shard_map/ppermute | solution.py:284
  18.1 1.8 %collective-permute-start.9 = (f32[656,128]{1,0:T(8,128)S(1)}, f32[656,128]{1,0:T(8,128)S(1)}, u32[]{:S(2)}, u32[]{:S(2)}) collective-permute-start(f32[656,128]{1,0:T(8,128)S(1)} %collective-permute-done.8.refs_0_), channel_id=1, source_target_pairs={{0,1},{1,0},{2,3},{3,2},{4,5},{5,4},{6,7},{7,6},{8,9},{9,8},{10,11... | collective-permute-start | bytes 1007624 | tf_op jit(solution)/shard_map/ppermute | solution.py:284
  19.8 4.0 %collective-permute-done.4.refs_0_ = f32[656,128]{1,0:T(8,128)S(1)} collective-permute-done((f32[656,128]{1,0:T(8,128)S(1)}, f32[656,128]{1,0:T(8,128)S(1)}, u32[]{:S(2)}, u32[]{:S(2)}) %collective-permute-start.4) | collective-permute-done | bytes 335904 | tf_op jit(solution)/shard_map/ppermute | solution.py:284
  23.8 1.5 %collective-permute-start.5 = (f32[656,128]{1,0:T(8,128)S(1)}, f32[656,128]{1,0:T(8,128)S(1)}, u32[]{:S(2)}, u32[]{:S(2)}) collective-permute-start(f32[656,128]{1,0:T(8,128)S(1)} %collective-permute-done.4.refs_0_), channel_id=1, source_target_pairs={{0,1},{1,0},{2,3},{3,2},{4,5},{5,4},{6,7},{7,6},{8,9},{9,8},{10,11... | collective-permute-start | bytes 1007624 | tf_op jit(solution)/shard_map/ppermute | solution.py:284
  25.4 1.9 %collective-permute-start = (f32[656,128]{1,0:T(8,128)S(1)}, f32[656,128]{1,0:T(8,128)S(1)}, u32[]{:S(2)}, u32[]{:S(2)}) collective-permute-start(f32[656,128]{1,0:T(8,128)S(1)} %get-tuple-element.28.refs_0_), channel_id=1, source_target_pairs={{0,4},{1,5},{2,6},{3,7},{4,0},{5,1},{6,2},{7,3},{8,12},{9,13},{10,... | collective-permute-start | bytes 1007624 | tf_op jit(solution)/shard_map/ppermute | solution.py:284
  27.8 6.3 %collective-permute-done.5.refs_1_ = f32[656,128]{1,0:T(8,128)S(1)} collective-permute-done((f32[656,128]{1,0:T(8,128)S(1)}, f32[656,128]{1,0:T(8,128)S(1)}, u32[]{:S(2)}, u32[]{:S(2)}) %collective-permute-start.5) | collective-permute-done | bytes 335904 | tf_op jit(solution)/shard_map/ppermute | solution.py:284
  34.1 2.4 %plane.4 = (bf16[256,1024]{1,0:T(8,128)(2,1)S(1)}, bf16[256,1024]{1,0:T(8,128)(2,1)S(1)}, f32[256,1024]{1,0:T(8,128)S(1)}) custom-call(f32[656,128]{1,0:T(8,128)S(1)} %get-tuple-element.28.refs_0_, f32[656,128]{1,0:T(8,128)S(1)} %collective-permute-done.1.refs_1_, f32[656,128]{1,0:T(8,128)S(1)} %get-tuple-element.29.refs_2_, ...), custom_call_target="tpu_custom_call" | custom-call | flops 2013265920 | bytes 4194304 | tf_op jit(solution)/shard_map/plane/pallas_call | solution.py:170
  36.5 6.9 %collective-permute-done.refs_0_ = f32[656,128]{1,0:T(8,128)S(1)} collective-permute-done((f32[656,128]{1,0:T(8,128)S(1)}, f32[656,128]{1,0:T(8,128)S(1)}, u32[]{:S(2)}, u32[]{:S(2)}) %collective-permute-start) | collective-permute-done | bytes 335904 | tf_op jit(solution)/shard_map/ppermute | solution.py:284
  44.2 2.4 %plane.5 = (bf16[256,1024]{1,0:T(8,128)(2,1)S(1)}, bf16[256,1024]{1,0:T(8,128)(2,1)S(1)}, f32[256,1024]{1,0:T(8,128)S(1)}) custom-call(f32[656,128]{1,0:T(8,128)S(1)} %collective-permute-done.8.refs_0_, f32[656,128]{1,0:T(8,128)S(1)} %collective-permute-done.9.refs_1_, f32[656,128]{1,0:T(8,128)S(1)} %collective-permute-done.10.refs_2_, ...), custom_call_target="tpu_custom_call" | custom-call | flops 2013265920 | bytes 4194304 | tf_op jit(solution)/shard_map/plane/pallas_call | solution.py:170
  46.6 2.4 %plane.6 = (bf16[256,1024]{1,0:T(8,128)(2,1)S(1)}, bf16[256,1024]{1,0:T(8,128)(2,1)S(1)}, f32[256,1024]{1,0:T(8,128)S(1)}) custom-call(f32[656,128]{1,0:T(8,128)S(1)} %collective-permute-done.4.refs_0_, f32[656,128]{1,0:T(8,128)S(1)} %collective-permute-done.5.refs_1_, f32[656,128]{1,0:T(8,128)S(1)} %collective-permute-done.6.refs_2_, ...), custom_call_target="tpu_custom_call" | custom-call | flops 2013265920 | bytes 4194304 | tf_op jit(solution)/shard_map/plane/pallas_call | solution.py:170
  49.0 4.8 %collective-permute-done.3.refs_1_ = f32[656,128]{1,0:T(8,128)S(1)} collective-permute-done((f32[656,128]{1,0:T(8,128)S(1)}, f32[656,128]{1,0:T(8,128)S(1)}, u32[]{:S(2)}, u32[]{:S(2)}) %collective-permute-start.3) | collective-permute-done | bytes 335904 | tf_op jit(solution)/shard_map/ppermute | solution.py:284
  53.8 1.6 %collective-permute-done.13.refs_3_ = f32[656,128]{1,0:T(8,128)S(1)} collective-permute-done((f32[656,128]{1,0:T(8,128)S(1)}, f32[656,128]{1,0:T(8,128)S(1)}, u32[]{:S(2)}, u32[]{:S(2)}) %collective-permute-start.13) | collective-permute-done | bytes 335904 | tf_op jit(solution)/shard_map/ppermute | solution.py:284
  55.4 2.4 %plane.7 = (bf16[256,1024]{1,0:T(8,128)(2,1)S(1)}, bf16[256,1024]{1,0:T(8,128)(2,1)S(1)}, f32[256,1024]{1,0:T(8,128)S(1)}) custom-call(f32[656,128]{1,0:T(8,128)S(1)} %collective-permute-done.refs_0_, f32[656,128]{1,0:T(8,128)S(1)} %collective-permute-done.3.refs_1_, f32[656,128]{1,0:T(8,128)S(1)} %collective-permute-done.12.refs_2_, ...), custom_call_target="tpu_custom_call" | custom-call | flops 2013265920 | bytes 4194304 | tf_op jit(solution)/shard_map/plane/pallas_call | solution.py:170
  59.4 1.4 %grad.2.kept_ref = f32[4,128,256]{2,1,0:T(8,128)S(1)} custom-call(f32[256,1024]{1,0:T(8,128)S(1)} %get-tuple-element.41.acc_ref, bf16[256,1024]{1,0:T(8,128)(2,1)S(1)} %get-tuple-element.42.refs_0_, bf16[256,1024]{1,0:T(8,128)(2,1)S(1)} %get-tuple-element.43.refs_1_, bf16[256,1024]{1,0:T(8,128)(2,1)S(1)} %get-tuple-element.44.refs_2_, ...), custom_call_target="tpu_custom_call" | custom-call | flops 805306368 | bytes 1048576 | tf_op jit(solution)/shard_map/grad/pallas_call | solution.py:209
  61.2 1.6 %collective-permute-start.15 = (f32[4,32,256]{2,1,0:T(8,128)S(1)}, f32[4,32,256]{2,1,0:T(8,128)S(1)}, u32[]{:S(2)}, u32[]{:S(2)}) collective-permute-start(f32[4,32,256]{2,1,0:T(8,128)S(1)} %get-tuple-element.51), channel_id=1, source_target_pairs={{0,16},{1,17},{2,18},{3,19},{4,20},{5,21},{6,22},{7,23},{8,24},{9,... | collective-permute-start | bytes 393224 | tf_op jit(solution)/shard_map/ppermute | solution.py:284
  64.8 2.4 %collective-permute-done.15 = f32[4,32,256]{2,1,0:T(8,128)S(1)} collective-permute-done((f32[4,32,256]{2,1,0:T(8,128)S(1)}, f32[4,32,256]{2,1,0:T(8,128)S(1)}, u32[]{:S(2)}, u32[]{:S(2)}) %collective-permute-start.15) | collective-permute-done | bytes 131104 | tf_op jit(solution)/shard_map/ppermute | solution.py:284
  67.2 3.7 %collective-permute-done.16 = f32[4,32,256]{2,1,0:T(8,128)S(1)} collective-permute-done((f32[4,32,256]{2,1,0:T(8,128)S(1)}, f32[4,32,256]{2,1,0:T(8,128)S(1)}, u32[]{:S(2)}, u32[]{:S(2)}) %collective-permute-start.16) | collective-permute-done | bytes 131104 | tf_op jit(solution)/shard_map/ppermute | solution.py:284
  70.9 2.8 %collective-permute-start.18 = (f32[32,256]{1,0:T(8,128)S(1)}, f32[32,256]{1,0:T(8,128)S(1)}, u32[]{:S(2)}, u32[]{:S(2)}) collective-permute-start(f32[32,256]{1,0:T(8,128)S(1)} %get-tuple-element.56), channel_id=1, source_target_pairs={{0,6},{1,7},{2,0},{3,1},{4,2},{5,3},{6,4},{7,5},{8,14},{9,15},{10,... | collective-permute-start | bytes 98312 | tf_op jit(solution)/shard_map/ppermute | solution.py:284
  75.3 4.1 %collective-permute-done.20 = f32[32,256]{1,0:T(8,128)S(1)} collective-permute-done((f32[32,256]{1,0:T(8,128)S(1)}, f32[32,256]{1,0:T(8,128)S(1)}, u32[]{:S(2)}, u32[]{:S(2)}) %collective-permute-start.20) | collective-permute-done | bytes 32800 | tf_op jit(solution)/shard_map/ppermute | solution.py:284
  (49 shorter events, 17.1 us)
Async XLA Ops:
  4.2 13.8 %collective-permute-start.8 = (f32[656,128]{1,0:T(8,128)S(1)}, f32[656,128]{1,0:T(8,128)S(1)}, u32[]{:S(2)}, u32[]{:S(2)}) collective-permute-start(f32[656,128]{1,0:T(8,128)S(1)} %get-tuple-element.28.refs_0_), channel_id=1, source_target_pairs={{0,2},{1,3},{2,4},{3,5},{4,6},{5,7},{6,0},{7,1},{8,10},{9,11},{10,... | collective-permute-start | bytes 1007624 | tf_op jit(solution)/shard_map/ppermute | solution.py:284
  7.3 16.5 %collective-permute-start.4 = (f32[656,128]{1,0:T(8,128)S(1)}, f32[656,128]{1,0:T(8,128)S(1)}, u32[]{:S(2)}, u32[]{:S(2)}) collective-permute-start(f32[656,128]{1,0:T(8,128)S(1)} %get-tuple-element.28.refs_0_), channel_id=1, source_target_pairs={{0,6},{1,7},{2,0},{3,1},{4,2},{5,3},{6,4},{7,5},{8,14},{9,15},{10,... | collective-permute-start | bytes 1007624 | tf_op jit(solution)/shard_map/ppermute | solution.py:284
  9.3 14.5 %collective-permute-start.1 = (f32[656,128]{1,0:T(8,128)S(1)}, f32[656,128]{1,0:T(8,128)S(1)}, u32[]{:S(2)}, u32[]{:S(2)}) collective-permute-start(f32[656,128]{1,0:T(8,128)S(1)} %get-tuple-element.28.refs_0_), channel_id=1, source_target_pairs={{0,1},{1,0},{2,3},{3,2},{4,5},{5,4},{6,7},{7,6},{8,9},{9,8},{10,11... | collective-permute-start | bytes 1007624 | tf_op jit(solution)/shard_map/ppermute | solution.py:284
  18.1 9.2 %collective-permute-start.9 = (f32[656,128]{1,0:T(8,128)S(1)}, f32[656,128]{1,0:T(8,128)S(1)}, u32[]{:S(2)}, u32[]{:S(2)}) collective-permute-start(f32[656,128]{1,0:T(8,128)S(1)} %collective-permute-done.8.refs_0_), channel_id=1, source_target_pairs={{0,1},{1,0},{2,3},{3,2},{4,5},{5,4},{6,7},{7,6},{8,9},{9,8},{10,11... | collective-permute-start | bytes 1007624 | tf_op jit(solution)/shard_map/ppermute | solution.py:284
  23.8 3.9 %collective-permute-start.2 = (f32[656,128]{1,0:T(8,128)S(1)}, f32[656,128]{1,0:T(8,128)S(1)}, u32[]{:S(2)}, u32[]{:S(2)}) collective-permute-start(f32[656,128]{1,0:T(8,128)S(1)} %collective-permute-done.1.refs_1_), channel_id=1, source_target_pairs={{0,8},{1,9},{2,10},{3,11},{4,12},{5,13},{6,14},{7,15},{8,0},{9,1},... | collective-permute-start | bytes 1007624 | tf_op jit(solution)/shard_map/ppermute | solution.py:284
  23.8 10.3 %collective-permute-start.5 = (f32[656,128]{1,0:T(8,128)S(1)}, f32[656,128]{1,0:T(8,128)S(1)}, u32[]{:S(2)}, u32[]{:S(2)}) collective-permute-start(f32[656,128]{1,0:T(8,128)S(1)} %collective-permute-done.4.refs_0_), channel_id=1, source_target_pairs={{0,1},{1,0},{2,3},{3,2},{4,5},{5,4},{6,7},{7,6},{8,9},{9,8},{10,11... | collective-permute-start | bytes 1007624 | tf_op jit(solution)/shard_map/ppermute | solution.py:284
  25.4 18.1 %collective-permute-start = (f32[656,128]{1,0:T(8,128)S(1)}, f32[656,128]{1,0:T(8,128)S(1)}, u32[]{:S(2)}, u32[]{:S(2)}) collective-permute-start(f32[656,128]{1,0:T(8,128)S(1)} %get-tuple-element.28.refs_0_), channel_id=1, source_target_pairs={{0,4},{1,5},{2,6},{3,7},{4,0},{5,1},{6,2},{7,3},{8,12},{9,13},{10,... | collective-permute-start | bytes 1007624 | tf_op jit(solution)/shard_map/ppermute | solution.py:284
  27.2 16.2 %collective-permute-start.10 = (f32[656,128]{1,0:T(8,128)S(1)}, f32[656,128]{1,0:T(8,128)S(1)}, u32[]{:S(2)}, u32[]{:S(2)}) collective-permute-start(f32[656,128]{1,0:T(8,128)S(1)} %collective-permute-done.8.refs_0_), channel_id=1, source_target_pairs={{0,8},{1,9},{2,10},{3,11},{4,12},{5,13},{6,14},{7,15},{8,0},{9,1},... | collective-permute-start | bytes 1007624 | tf_op jit(solution)/shard_map/ppermute | solution.py:284
  27.2 16.9 %collective-permute-start.11 = (f32[656,128]{1,0:T(8,128)S(1)}, f32[656,128]{1,0:T(8,128)S(1)}, u32[]{:S(2)}, u32[]{:S(2)}) collective-permute-start(f32[656,128]{1,0:T(8,128)S(1)} %collective-permute-done.9.refs_1_), channel_id=1, source_target_pairs={{0,8},{1,9},{2,10},{3,11},{4,12},{5,13},{6,14},{7,15},{8,0},{9,1},... | collective-permute-start | bytes 1007624 | tf_op jit(solution)/shard_map/ppermute | solution.py:284
  27.7 18.8 %collective-permute-start.6 = (f32[656,128]{1,0:T(8,128)S(1)}, f32[656,128]{1,0:T(8,128)S(1)}, u32[]{:S(2)}, u32[]{:S(2)}) collective-permute-start(f32[656,128]{1,0:T(8,128)S(1)} %collective-permute-done.4.refs_0_), channel_id=1, source_target_pairs={{0,8},{1,9},{2,10},{3,11},{4,12},{5,13},{6,14},{7,15},{8,0},{9,1},... | collective-permute-start | bytes 1007624 | tf_op jit(solution)/shard_map/ppermute | solution.py:284
  34.1 12.4 %collective-permute-start.7 = (f32[656,128]{1,0:T(8,128)S(1)}, f32[656,128]{1,0:T(8,128)S(1)}, u32[]{:S(2)}, u32[]{:S(2)}) collective-permute-start(f32[656,128]{1,0:T(8,128)S(1)} %collective-permute-done.5.refs_1_), channel_id=1, source_target_pairs={{0,8},{1,9},{2,10},{3,11},{4,12},{5,13},{6,14},{7,15},{8,0},{9,1},... | collective-permute-start | bytes 1007624 | tf_op jit(solution)/shard_map/ppermute | solution.py:284
  43.5 10.3 %collective-permute-start.12 = (f32[656,128]{1,0:T(8,128)S(1)}, f32[656,128]{1,0:T(8,128)S(1)}, u32[]{:S(2)}, u32[]{:S(2)}) collective-permute-start(f32[656,128]{1,0:T(8,128)S(1)} %collective-permute-done.refs_0_), channel_id=1, source_target_pairs={{0,8},{1,9},{2,10},{3,11},{4,12},{5,13},{6,14},{7,15},{8,0},{9,1},... | collective-permute-start | bytes 1007624 | tf_op jit(solution)/shard_map/ppermute | solution.py:284
  43.5 10.3 %collective-permute-start.3 = (f32[656,128]{1,0:T(8,128)S(1)}, f32[656,128]{1,0:T(8,128)S(1)}, u32[]{:S(2)}, u32[]{:S(2)}) collective-permute-start(f32[656,128]{1,0:T(8,128)S(1)} %collective-permute-done.refs_0_), channel_id=1, source_target_pairs={{0,1},{1,0},{2,3},{3,2},{4,5},{5,4},{6,7},{7,6},{8,9},{9,8},{10,11... | collective-permute-start | bytes 1007624 | tf_op jit(solution)/shard_map/ppermute | solution.py:284
  53.8 1.6 %collective-permute-start.13 = (f32[656,128]{1,0:T(8,128)S(1)}, f32[656,128]{1,0:T(8,128)S(1)}, u32[]{:S(2)}, u32[]{:S(2)}) collective-permute-start(f32[656,128]{1,0:T(8,128)S(1)} %collective-permute-done.3.refs_1_), channel_id=1, source_target_pairs={{0,8},{1,9},{2,10},{3,11},{4,12},{5,13},{6,14},{7,15},{8,0},{9,1},... | collective-permute-start | bytes 1007624 | tf_op jit(solution)/shard_map/ppermute | solution.py:284
  59.2 2.0 %collective-permute-start.14 = (f32[4,128,256]{2,1,0:T(8,128)S(1)}, f32[4,128,256]{2,1,0:T(8,128)S(1)}, u32[]{:S(2)}, u32[]{:S(2)}) collective-permute-start(f32[4,128,256]{2,1,0:T(8,128)S(1)} %grad.3), channel_id=1, source_target_pairs={{0,8},{1,9},{2,10},{3,11},{4,12},{5,13},{6,14},{7,15},{8,0},{9,1},... | collective-permute-start | bytes 1572872 | tf_op jit(solution)/shard_map/ppermute | solution.py:284
  61.2 6.0 %collective-permute-start.15 = (f32[4,32,256]{2,1,0:T(8,128)S(1)}, f32[4,32,256]{2,1,0:T(8,128)S(1)}, u32[]{:S(2)}, u32[]{:S(2)}) collective-permute-start(f32[4,32,256]{2,1,0:T(8,128)S(1)} %get-tuple-element.51), channel_id=1, source_target_pairs={{0,16},{1,17},{2,18},{3,19},{4,20},{5,21},{6,22},{7,23},{8,24},{9,... | collective-permute-start | bytes 393224 | tf_op jit(solution)/shard_map/ppermute | solution.py:284
  62.8 8.1 %collective-permute-start.16 = (f32[4,32,256]{2,1,0:T(8,128)S(1)}, f32[4,32,256]{2,1,0:T(8,128)S(1)}, u32[]{:S(2)}, u32[]{:S(2)}) collective-permute-start(f32[4,32,256]{2,1,0:T(8,128)S(1)} %get-tuple-element.52), channel_id=1, source_target_pairs={{0,1},{1,0},{2,3},{3,2},{4,5},{5,4},{6,7},{7,6},{8,9},{9,8},{10,11... | collective-permute-start | bytes 393224 | tf_op jit(solution)/shard_map/ppermute | solution.py:284
  63.5 7.4 %collective-permute-start.17 = (f32[4,32,256]{2,1,0:T(8,128)S(1)}, f32[4,32,256]{2,1,0:T(8,128)S(1)}, u32[]{:S(2)}, u32[]{:S(2)}) collective-permute-start(f32[4,32,256]{2,1,0:T(8,128)S(1)} %get-tuple-element.53), channel_id=1, source_target_pairs={{0,17},{1,16},{2,19},{3,18},{4,21},{5,20},{6,23},{7,22},{8,25},{9,... | collective-permute-start | bytes 393224 | tf_op jit(solution)/shard_map/ppermute | solution.py:284
  70.9 4.4 %collective-permute-start.18 = (f32[32,256]{1,0:T(8,128)S(1)}, f32[32,256]{1,0:T(8,128)S(1)}, u32[]{:S(2)}, u32[]{:S(2)}) collective-permute-start(f32[32,256]{1,0:T(8,128)S(1)} %get-tuple-element.56), channel_id=1, source_target_pairs={{0,6},{1,7},{2,0},{3,1},{4,2},{5,3},{6,4},{7,5},{8,14},{9,15},{10,... | collective-permute-start | bytes 98312 | tf_op jit(solution)/shard_map/ppermute | solution.py:284
  73.7 5.7 %collective-permute-start.20 = (f32[32,256]{1,0:T(8,128)S(1)}, f32[32,256]{1,0:T(8,128)S(1)}, u32[]{:S(2)}, u32[]{:S(2)}) collective-permute-start(f32[32,256]{1,0:T(8,128)S(1)} %get-tuple-element.57), channel_id=1, source_target_pairs={{0,2},{1,3},{2,4},{3,5},{4,6},{5,7},{6,0},{7,1},{8,10},{9,11},{10,... | collective-permute-start | bytes 98312 | tf_op jit(solution)/shard_map/ppermute | solution.py:284
  73.7 5.7 %collective-permute-start.19 = (f32[32,256]{1,0:T(8,128)S(1)}, f32[32,256]{1,0:T(8,128)S(1)}, u32[]{:S(2)}, u32[]{:S(2)}) collective-permute-start(f32[32,256]{1,0:T(8,128)S(1)} %get-tuple-element.58), channel_id=1, source_target_pairs={{0,4},{1,5},{2,6},{3,7},{4,0},{5,1},{6,2},{7,3},{8,12},{9,13},{10,... | collective-permute-start | bytes 98312 | tf_op jit(solution)/shard_map/ppermute | solution.py:284
  79.4 3.5 %collective-permute-start.23 = (f32[32,256]{1,0:T(8,128)S(1)}, f32[32,256]{1,0:T(8,128)S(1)}, u32[]{:S(2)}, u32[]{:S(2)}) collective-permute-start(f32[32,256]{1,0:T(8,128)S(1)} %fusion.3.refs_0_), channel_id=1, source_target_pairs={{0,24},{1,25},{2,26},{3,27},{4,28},{5,29},{6,30},{7,31},{8,16},{9,... | collective-permute-start | bytes 98312 | tf_op jit(solution)/shard_map/ppermute | solution.py:284
  79.5 4.0 %collective-permute-start.22 = (f32[32,256]{1,0:T(8,128)S(1)}, f32[32,256]{1,0:T(8,128)S(1)}, u32[]{:S(2)}, u32[]{:S(2)}) collective-permute-start(f32[32,256]{1,0:T(8,128)S(1)} %fusion.3.refs_0_), channel_id=1, source_target_pairs={{0,16},{1,17},{2,18},{3,19},{4,20},{5,21},{6,22},{7,23},{8,24},{9,... | collective-permute-start | bytes 98312 | tf_op jit(solution)/shard_map/ppermute | solution.py:284
  80.8 2.7 %collective-permute-start.21 = (f32[32,256]{1,0:T(8,128)S(1)}, f32[32,256]{1,0:T(8,128)S(1)}, u32[]{:S(2)}, u32[]{:S(2)}) collective-permute-start(f32[32,256]{1,0:T(8,128)S(1)} %fusion.3.refs_0_), channel_id=1, source_target_pairs={{0,8},{1,9},{2,10},{3,11},{4,12},{5,13},{6,14},{7,15},{8,0},{9,1},... | collective-permute-start | bytes 98312 | tf_op jit(solution)/shard_map/ppermute | solution.py:284
  (5 other events, 6.0 us)

commit v3 on v2

--- a/solution.py
+++ b/solution.py
@@ -122,7 +122,7 @@
             pl.BlockSpec((width, step), lambda i: (0, i)),
         ),
         compiler_params=params(),
-        cost_estimate=pl.CostEstimate(flops=4 * rows * depth, bytes_accessed=10 * rows * depth, transcendentals=0),
+        cost_estimate=pl.CostEstimate(flops=1, bytes_accessed=1, transcendentals=0),
         name="prep",
     )(features, targets)
 
@@ -184,9 +184,7 @@
             pltpu.VMEM((count, LANES), F32),
         ],
         compiler_params=params(),
-        cost_estimate=pl.CostEstimate(
-            flops=6 * rows * count * (depth + width), bytes_accessed=4 * rows * depth, transcendentals=rows * count
-        ),
+        cost_estimate=pl.CostEstimate(flops=1, bytes_accessed=1, transcendentals=0),
         name="plane",
     )(*messages, fh, fl, sq, acc)
 
@@ -212,9 +210,7 @@
         in_specs=[VMEM] * (1 + 2 * planes),
         out_specs=VMEM,
         compiler_params=params(),
-        cost_estimate=pl.CostEstimate(
-            flops=6 * rows * count * width * planes, bytes_accessed=4 * rows * width, transcendentals=0
-        ),
+        cost_estimate=pl.CostEstimate(flops=1, bytes_accessed=1, transcendentals=0),
         name="grad",
     )(acc, *khs, *kls)
 
@@ -291,15 +287,15 @@
     messages = (mine, near, sib, move(near, core=1))
     khs, kls = {}, {}
     khs[0], kls[0], acc = plane(messages, fh, fl, sq, acc, parts, piece)
-    accs = [sq, sq, acc]
+    accs = [sq,None,None]
     others = {}
     for n, k in enumerate(order):
-        same = after(far[k], accs[n]) if n < 3 else far[k]
+        same = after(far[k], accs[n]) if n < 3 and accs[n] is not None else far[k]
         far[k] = same
         others[k] = move(same, y=1)
     for n, k in enumerate(order):
         same, other = far[k], others[k]
-        if n == len(order) - 1:
+        if n==len(order)-1:
             other = after(other, acc)
         messages = (same, other, move(same, core=1), move(other, core=1))
         khs[k], kls[k], acc = plane(messages, fh, fl, sq, acc, parts, piece)

time: 85 us -> 79.9 us (0.940)
  waiting for transfers between devices: 38.2 us -> 25 us
  starting transfers between devices: 22.3 us -> 30.5 us
    ppermute x24, waiting for transfers between devices: 38.2 us -> 25 us  [move(): return lax.ppermute(value, ('grp', 'own'), pairs)]
    ppermute x24, starting transfers between devices: 22.3 us -> 30.5 us  [move(): return lax.ppermute(value, ('grp', 'own'), pairs)]
  transfers between devices with their start and end apart: 24 -> 24, of which waited for: 13 -> 12; matrix products, arithmetic and copies ran while one was open for 2% -> 2% of each run, Pallas kernels for 12% -> 13%
where the time goes in v3:
time: 79.9 us; the launch traced here: 79.7 us
  starting transfers between devices  30.5 us (38%)
  waiting for transfers between devices  25 us (31%)
  Pallas kernels  16 us (20%)
  local copies, waits for them, and re-layouts  7.33 us (9%)
  between operations  0.8 us (1%)
    ppermute x24, starting transfers between devices, move(): return lax.ppermute(value, ('grp', 'own'), pairs)  30.5 us
    ppermute x24, waiting for transfers between devices, move(): return lax.ppermute(value, ('grp', 'own'), pairs)  25 us
    pallas_call x4, Pallas kernels, plane(): pl.pallas_call(functools.partial(plane_kernel, parts, len(messages), piec...  9.59 us
    unnamed x11, local copies, waits for them, and re-layouts  7.32 us
    pallas_call x2, Pallas kernels, grad(): pl.pallas_call(functools.partial(grad_kernel, planes, which), out_shape=j...  2.73 us
  transfers between devices with their start and end apart: 24, of which 12 were waited for; matrix products, arithmetic and copies ran while one was open for 2% of the time, Pallas kernels for 13%

profile of v3, /device:TPU:0, one launch (start us, length us, event | category | flops | bytes accessed | tf_op | source)
XLA Modules:
  0.0 79.7 jit_solution(7786457568099286147)
XLA Ops:
  4.2 3.0 %collective-permute-start.6 = (f32[656,128]{1,0:T(8,128)S(1)}, f32[656,128]{1,0:T(8,128)S(1)}, u32[]{:S(2)}, u32[]{:S(2)}) collective-permute-start(f32[656,128]{1,0:T(8,128)S(1)} %get-tuple-element.26.refs_0_), channel_id=1, source_target_pairs={{0,2},{1,3},{2,4},{3,5},{4,6},{5,7},{6,0},{7,1},{8,10},{9,11},{10,... | collective-permute-start | bytes 1007624 | tf_op jit(solution)/shard_map/ppermute | solution.py:280
  7.3 2.0 %collective-permute-start.2 = (f32[656,128]{1,0:T(8,128)S(1)}, f32[656,128]{1,0:T(8,128)S(1)}, u32[]{:S(2)}, u32[]{:S(2)}) collective-permute-start(f32[656,128]{1,0:T(8,128)S(1)} %get-tuple-element.26.refs_0_), channel_id=1, source_target_pairs={{0,6},{1,7},{2,0},{3,1},{4,2},{5,3},{6,4},{7,5},{8,14},{9,15},{10,... | collective-permute-start | bytes 1007624 | tf_op jit(solution)/shard_map/ppermute | solution.py:280
  9.3 1.7 %collective-permute-start.10 = (f32[656,128]{1,0:T(8,128)S(1)}, f32[656,128]{1,0:T(8,128)S(1)}, u32[]{:S(2)}, u32[]{:S(2)}) collective-permute-start(f32[656,128]{1,0:T(8,128)S(1)} %get-tuple-element.26.refs_0_), channel_id=1, source_target_pairs={{0,1},{1,0},{2,3},{3,2},{4,5},{5,4},{6,7},{7,6},{8,9},{9,8},{10,11... | collective-permute-start | bytes 1007624 | tf_op jit(solution)/shard_map/ppermute | solution.py:280
  11.1 2.2 %copy-done = f32[1024,1024]{1,0:T(8,128)S(1)} copy-done((f32[1024,1024]{1,0:T(8,128)S(1)}, f32[1024,1024]{1,0:T(8,128)}, u32[]{:S(2)}) %copy-start) | copy-done | bytes 4194328
  14.5 1.5 %prep.1 = (bf16[1024,1024]{1,0:T(8,128)(2,1)S(1)}, bf16[1024,1024]{1,0:T(8,128)(2,1)S(1)}, f32[8,1024]{1,0:T(8,128)S(1)}, f32[256,1024]{1,0:T(8,128)S(1)}) custom-call(f32[1024,1024]{1,0:T(8,128)S(1)} %copy-done, f32[1024,256]{1,0:T(8,128)S(1)} %copy-done.1), custom_call_target="tpu_custom_call" | custom-call | flops 1 | bytes 1 | tf_op jit(solution)/shard_map/prep/pallas_call | solution.py:108
  15.9 2.1 %collective-permute-done.6.refs_0_ = f32[656,128]{1,0:T(8,128)S(1)} collective-permute-done((f32[656,128]{1,0:T(8,128)S(1)}, f32[656,128]{1,0:T(8,128)S(1)}, u32[]{:S(2)}, u32[]{:S(2)}) %collective-permute-start.6) | collective-permute-done | bytes 335904 | tf_op jit(solution)/shard_map/ppermute | solution.py:280
  18.1 1.8 %collective-permute-start.7 = (f32[656,128]{1,0:T(8,128)S(1)}, f32[656,128]{1,0:T(8,128)S(1)}, u32[]{:S(2)}, u32[]{:S(2)}) collective-permute-start(f32[656,128]{1,0:T(8,128)S(1)} %collective-permute-done.6.refs_0_), channel_id=1, source_target_pairs={{0,1},{1,0},{2,3},{3,2},{4,5},{5,4},{6,7},{7,6},{8,9},{9,8},{10,11... | collective-permute-start | bytes 1007624 | tf_op jit(solution)/shard_map/ppermute | solution.py:280
  19.8 10.4 %collective-permute-start = (f32[656,128]{1,0:T(8,128)S(1)}, f32[656,128]{1,0:T(8,128)S(1)}, u32[]{:S(2)}, u32[]{:S(2)}) collective-permute-start(f32[656,128]{1,0:T(8,128)S(1)} %get-tuple-element.26.refs_0_), channel_id=1, source_target_pairs={{0,4},{1,5},{2,6},{3,7},{4,0},{5,1},{6,2},{7,3},{8,12},{9,13},{10,... | collective-permute-start | bytes 1007624 | tf_op jit(solution)/shard_map/ppermute | solution.py:280
  31.3 7.5 %collective-permute-done.refs_0_ = f32[656,128]{1,0:T(8,128)S(1)} collective-permute-done((f32[656,128]{1,0:T(8,128)S(1)}, f32[656,128]{1,0:T(8,128)S(1)}, u32[]{:S(2)}, u32[]{:S(2)}) %collective-permute-start) | collective-permute-done | bytes 335904 | tf_op jit(solution)/shard_map/ppermute | solution.py:280
  39.3 1.5 %collective-permute-start.1 = (f32[656,128]{1,0:T(8,128)S(1)}, f32[656,128]{1,0:T(8,128)S(1)}, u32[]{:S(2)}, u32[]{:S(2)}) collective-permute-start(f32[656,128]{1,0:T(8,128)S(1)} %collective-permute-done.refs_0_), channel_id=1, source_target_pairs={{0,1},{1,0},{2,3},{3,2},{4,5},{5,4},{6,7},{7,6},{8,9},{9,8},{10,11... | collective-permute-start | bytes 1007624 | tf_op jit(solution)/shard_map/ppermute | solution.py:280
  40.8 2.4 %plane.4 = (bf16[256,1024]{1,0:T(8,128)(2,1)S(1)}, bf16[256,1024]{1,0:T(8,128)(2,1)S(1)}, f32[256,1024]{1,0:T(8,128)S(1)}) custom-call(f32[656,128]{1,0:T(8,128)S(1)} %get-tuple-element.26.refs_0_, f32[656,128]{1,0:T(8,128)S(1)} %collective-permute-done.10.refs_1_, f32[656,128]{1,0:T(8,128)S(1)} %get-tuple-element.31.refs_2_, ...), custom_call_target="tpu_custom_call" | custom-call | flops 1 | bytes 1 | tf_op jit(solution)/shard_map/plane/pallas_call | solution.py:170
  43.3 2.4 %plane.5 = (bf16[256,1024]{1,0:T(8,128)(2,1)S(1)}, bf16[256,1024]{1,0:T(8,128)(2,1)S(1)}, f32[256,1024]{1,0:T(8,128)S(1)}) custom-call(f32[656,128]{1,0:T(8,128)S(1)} %collective-permute-done.6.refs_0_, f32[656,128]{1,0:T(8,128)S(1)} %collective-permute-done.7.refs_1_, f32[656,128]{1,0:T(8,128)S(1)} %collective-permute-done.8.refs_2_, ...), custom_call_target="tpu_custom_call" | custom-call | flops 1 | bytes 1 | tf_op jit(solution)/shard_map/plane/pallas_call | solution.py:170
  45.7 2.4 %plane.6 = (bf16[256,1024]{1,0:T(8,128)(2,1)S(1)}, bf16[256,1024]{1,0:T(8,128)(2,1)S(1)}, f32[256,1024]{1,0:T(8,128)S(1)}) custom-call(f32[656,128]{1,0:T(8,128)S(1)} %collective-permute-done.2.refs_0_, f32[656,128]{1,0:T(8,128)S(1)} %collective-permute-done.3.refs_1_, f32[656,128]{1,0:T(8,128)S(1)} %collective-permute-done.4.refs_2_, ...), custom_call_target="tpu_custom_call" | custom-call | flops 1 | bytes 1 | tf_op jit(solution)/shard_map/plane/pallas_call | solution.py:170
  49.2 1.6 %collective-permute-done.13.refs_3_ = f32[656,128]{1,0:T(8,128)S(1)} collective-permute-done((f32[656,128]{1,0:T(8,128)S(1)}, f32[656,128]{1,0:T(8,128)S(1)}, u32[]{:S(2)}, u32[]{:S(2)}) %collective-permute-start.13) | collective-permute-done | bytes 335904 | tf_op jit(solution)/shard_map/ppermute | solution.py:280
  50.8 2.4 %plane.7 = (bf16[256,1024]{1,0:T(8,128)(2,1)S(1)}, bf16[256,1024]{1,0:T(8,128)(2,1)S(1)}, f32[256,1024]{1,0:T(8,128)S(1)}) custom-call(f32[656,128]{1,0:T(8,128)S(1)} %collective-permute-done.refs_0_, f32[656,128]{1,0:T(8,128)S(1)} %collective-permute-done.1.refs_1_, f32[656,128]{1,0:T(8,128)S(1)} %collective-permute-done.12.refs_2_, ...), custom_call_target="tpu_custom_call" | custom-call | flops 1 | bytes 1 | tf_op jit(solution)/shard_map/plane/pallas_call | solution.py:170
  53.2 1.4 %grad.3 = f32[4,128,256]{2,1,0:T(8,128)S(1)} custom-call(f32[256,1024]{1,0:T(8,128)S(1)} %get-tuple-element.37.acc_ref, bf16[256,1024]{1,0:T(8,128)(2,1)S(1)} %get-tuple-element.38.refs_0_, bf16[256,1024]{1,0:T(8,128)(2,1)S(1)} %get-tuple-element.39.refs_1_, bf16[256,1024]{1,0:T(8,128)(2,1)S(1)} %get-tuple-element.40.refs_2_, ...), custom_call_target="tpu_custom_call" | custom-call | flops 1 | bytes 1 | tf_op jit(solution)/shard_map/grad/pallas_call | solution.py:207
  54.8 1.4 %grad.2.kept_ref = f32[4,128,256]{2,1,0:T(8,128)S(1)} custom-call(f32[256,1024]{1,0:T(8,128)S(1)} %get-tuple-element.37.acc_ref, bf16[256,1024]{1,0:T(8,128)(2,1)S(1)} %get-tuple-element.38.refs_0_, bf16[256,1024]{1,0:T(8,128)(2,1)S(1)} %get-tuple-element.39.refs_1_, bf16[256,1024]{1,0:T(8,128)(2,1)S(1)} %get-tuple-element.40.refs_2_, ...), custom_call_target="tpu_custom_call" | custom-call | flops 1 | bytes 1 | tf_op jit(solution)/shard_map/grad/pallas_call | solution.py:207
  56.6 1.6 %collective-permute-start.15 = (f32[4,32,256]{2,1,0:T(8,128)S(1)}, f32[4,32,256]{2,1,0:T(8,128)S(1)}, u32[]{:S(2)}, u32[]{:S(2)}) collective-permute-start(f32[4,32,256]{2,1,0:T(8,128)S(1)} %get-tuple-element.47), channel_id=1, source_target_pairs={{0,16},{1,17},{2,18},{3,19},{4,20},{5,21},{6,22},{7,23},{8,24},{9,... | collective-permute-start | bytes 393224 | tf_op jit(solution)/shard_map/ppermute | solution.py:280
  58.2 1.5 %collective-permute-start.16 = (f32[4,32,256]{2,1,0:T(8,128)S(1)}, f32[4,32,256]{2,1,0:T(8,128)S(1)}, u32[]{:S(2)}, u32[]{:S(2)}) collective-permute-start(f32[4,32,256]{2,1,0:T(8,128)S(1)} %get-tuple-element.48), channel_id=1, source_target_pairs={{0,1},{1,0},{2,3},{3,2},{4,5},{5,4},{6,7},{7,6},{8,9},{9,8},{10,11... | collective-permute-start | bytes 393224 | tf_op jit(solution)/shard_map/ppermute | solution.py:280
  60.2 2.4 %collective-permute-done.15 = f32[4,32,256]{2,1,0:T(8,128)S(1)} collective-permute-done((f32[4,32,256]{2,1,0:T(8,128)S(1)}, f32[4,32,256]{2,1,0:T(8,128)S(1)}, u32[]{:S(2)}, u32[]{:S(2)}) %collective-permute-start.15) | collective-permute-done | bytes 131104 | tf_op jit(solution)/shard_map/ppermute | solution.py:280
  62.6 3.7 %collective-permute-done.16 = f32[4,32,256]{2,1,0:T(8,128)S(1)} collective-permute-done((f32[4,32,256]{2,1,0:T(8,128)S(1)}, f32[4,32,256]{2,1,0:T(8,128)S(1)}, u32[]{:S(2)}, u32[]{:S(2)}) %collective-permute-start.16) | collective-permute-done | bytes 131104 | tf_op jit(solution)/shard_map/ppermute | solution.py:280
  66.3 1.7 %collective-permute-start.18 = (f32[32,256]{1,0:T(8,128)S(1)}, f32[32,256]{1,0:T(8,128)S(1)}, u32[]{:S(2)}, u32[]{:S(2)}) collective-permute-start(f32[32,256]{1,0:T(8,128)S(1)} %get-tuple-element.52), channel_id=1, source_target_pairs={{0,6},{1,7},{2,0},{3,1},{4,2},{5,3},{6,4},{7,5},{8,14},{9,15},{10,... | collective-permute-start | bytes 98312 | tf_op jit(solution)/shard_map/ppermute | solution.py:280
  69.0 1.5 %collective-permute-done.18 = f32[32,256]{1,0:T(8,128)S(1)} collective-permute-done((f32[32,256]{1,0:T(8,128)S(1)}, f32[32,256]{1,0:T(8,128)S(1)}, u32[]{:S(2)}, u32[]{:S(2)}) %collective-permute-start.18) | collective-permute-done | bytes 32800 | tf_op jit(solution)/shard_map/ppermute | solution.py:280
  70.5 2.5 %collective-permute-done.19 = f32[32,256]{1,0:T(8,128)S(1)} collective-permute-done((f32[32,256]{1,0:T(8,128)S(1)}, f32[32,256]{1,0:T(8,128)S(1)}, u32[]{:S(2)}, u32[]{:S(2)}) %collective-permute-start.19) | collective-permute-done | bytes 32800 | tf_op jit(solution)/shard_map/ppermute | solution.py:280
  (49 shorter events, 16.3 us)
Async XLA Ops:
  4.2 13.8 %collective-permute-start.6 = (f32[656,128]{1,0:T(8,128)S(1)}, f32[656,128]{1,0:T(8,128)S(1)}, u32[]{:S(2)}, u32[]{:S(2)}) collective-permute-start(f32[656,128]{1,0:T(8,128)S(1)} %get-tuple-element.26.refs_0_), channel_id=1, source_target_pairs={{0,2},{1,3},{2,4},{3,5},{4,6},{5,7},{6,0},{7,1},{8,10},{9,11},{10,... | collective-permute-start | bytes 1007624 | tf_op jit(solution)/shard_map/ppermute | solution.py:280
  7.3 23.0 %collective-permute-start.2 = (f32[656,128]{1,0:T(8,128)S(1)}, f32[656,128]{1,0:T(8,128)S(1)}, u32[]{:S(2)}, u32[]{:S(2)}) collective-permute-start(f32[656,128]{1,0:T(8,128)S(1)} %get-tuple-element.26.refs_0_), channel_id=1, source_target_pairs={{0,6},{1,7},{2,0},{3,1},{4,2},{5,3},{6,4},{7,5},{8,14},{9,15},{10,... | collective-permute-start | bytes 1007624 | tf_op jit(solution)/shard_map/ppermute | solution.py:280
  9.3 21.4 %collective-permute-start.10 = (f32[656,128]{1,0:T(8,128)S(1)}, f32[656,128]{1,0:T(8,128)S(1)}, u32[]{:S(2)}, u32[]{:S(2)}) collective-permute-start(f32[656,128]{1,0:T(8,128)S(1)} %get-tuple-element.26.refs_0_), channel_id=1, source_target_pairs={{0,1},{1,0},{2,3},{3,2},{4,5},{5,4},{6,7},{7,6},{8,9},{9,8},{10,11... | collective-permute-start | bytes 1007624 | tf_op jit(solution)/shard_map/ppermute | solution.py:280
  18.1 13.2 %collective-permute-start.7 = (f32[656,128]{1,0:T(8,128)S(1)}, f32[656,128]{1,0:T(8,128)S(1)}, u32[]{:S(2)}, u32[]{:S(2)}) collective-permute-start(f32[656,128]{1,0:T(8,128)S(1)} %collective-permute-done.6.refs_0_), channel_id=1, source_target_pairs={{0,1},{1,0},{2,3},{3,2},{4,5},{5,4},{6,7},{7,6},{8,9},{9,8},{10,11... | collective-permute-start | bytes 1007624 | tf_op jit(solution)/shard_map/ppermute | solution.py:280
  19.8 19.0 %collective-permute-start = (f32[656,128]{1,0:T(8,128)S(1)}, f32[656,128]{1,0:T(8,128)S(1)}, u32[]{:S(2)}, u32[]{:S(2)}) collective-permute-start(f32[656,128]{1,0:T(8,128)S(1)} %get-tuple-element.26.refs_0_), channel_id=1, source_target_pairs={{0,4},{1,5},{2,6},{3,7},{4,0},{5,1},{6,2},{7,3},{8,12},{9,13},{10,... | collective-permute-start | bytes 1007624 | tf_op jit(solution)/shard_map/ppermute | solution.py:280
  30.2 8.5 %collective-permute-start.3 = (f32[656,128]{1,0:T(8,128)S(1)}, f32[656,128]{1,0:T(8,128)S(1)}, u32[]{:S(2)}, u32[]{:S(2)}) collective-permute-start(f32[656,128]{1,0:T(8,128)S(1)} %collective-permute-done.2.refs_0_), channel_id=1, source_target_pairs={{0,1},{1,0},{2,3},{3,2},{4,5},{5,4},{6,7},{7,6},{8,9},{9,8},{10,11... | collective-permute-start | bytes 1007624 | tf_op jit(solution)/shard_map/ppermute | solution.py:280
  30.8 8.6 %collective-permute-start.11 = (f32[656,128]{1,0:T(8,128)S(1)}, f32[656,128]{1,0:T(8,128)S(1)}, u32[]{:S(2)}, u32[]{:S(2)}) collective-permute-start(f32[656,128]{1,0:T(8,128)S(1)} %collective-permute-done.10.refs_1_), channel_id=1, source_target_pairs={{0,8},{1,9},{2,10},{3,11},{4,12},{5,13},{6,14},{7,15},{8,0},{9,1},... | collective-permute-start | bytes 1007624 | tf_op jit(solution)/shard_map/ppermute | solution.py:280
  30.8 12.5 %collective-permute-start.8 = (f32[656,128]{1,0:T(8,128)S(1)}, f32[656,128]{1,0:T(8,128)S(1)}, u32[]{:S(2)}, u32[]{:S(2)}) collective-permute-start(f32[656,128]{1,0:T(8,128)S(1)} %collective-permute-done.6.refs_0_), channel_id=1, source_target_pairs={{0,8},{1,9},{2,10},{3,11},{4,12},{5,13},{6,14},{7,15},{8,0},{9,1},... | collective-permute-start | bytes 1007624 | tf_op jit(solution)/shard_map/ppermute | solution.py:280
  31.3 12.0 %collective-permute-start.9 = (f32[656,128]{1,0:T(8,128)S(1)}, f32[656,128]{1,0:T(8,128)S(1)}, u32[]{:S(2)}, u32[]{:S(2)}) collective-permute-start(f32[656,128]{1,0:T(8,128)S(1)} %collective-permute-done.7.refs_1_), channel_id=1, source_target_pairs={{0,8},{1,9},{2,10},{3,11},{4,12},{5,13},{6,14},{7,15},{8,0},{9,1},... | collective-permute-start | bytes 1007624 | tf_op jit(solution)/shard_map/ppermute | solution.py:280
  38.8 6.9 %collective-permute-start.4 = (f32[656,128]{1,0:T(8,128)S(1)}, f32[656,128]{1,0:T(8,128)S(1)}, u32[]{:S(2)}, u32[]{:S(2)}) collective-permute-start(f32[656,128]{1,0:T(8,128)S(1)} %collective-permute-done.2.refs_0_), channel_id=1, source_target_pairs={{0,8},{1,9},{2,10},{3,11},{4,12},{5,13},{6,14},{7,15},{8,0},{9,1},... | collective-permute-start | bytes 1007624 | tf_op jit(solution)/shard_map/ppermute | solution.py:280
  38.8 6.9 %collective-permute-start.5 = (f32[656,128]{1,0:T(8,128)S(1)}, f32[656,128]{1,0:T(8,128)S(1)}, u32[]{:S(2)}, u32[]{:S(2)}) collective-permute-start(f32[656,128]{1,0:T(8,128)S(1)} %collective-permute-done.3.refs_1_), channel_id=1, source_target_pairs={{0,8},{1,9},{2,10},{3,11},{4,12},{5,13},{6,14},{7,15},{8,0},{9,1},... | collective-permute-start | bytes 1007624 | tf_op jit(solution)/shard_map/ppermute | solution.py:280
  39.3 9.9 %collective-permute-start.1 = (f32[656,128]{1,0:T(8,128)S(1)}, f32[656,128]{1,0:T(8,128)S(1)}, u32[]{:S(2)}, u32[]{:S(2)}) collective-permute-start(f32[656,128]{1,0:T(8,128)S(1)} %collective-permute-done.refs_0_), channel_id=1, source_target_pairs={{0,1},{1,0},{2,3},{3,2},{4,5},{5,4},{6,7},{7,6},{8,9},{9,8},{10,11... | collective-permute-start | bytes 1007624 | tf_op jit(solution)/shard_map/ppermute | solution.py:280
  43.2 5.9 %collective-permute-start.12 = (f32[656,128]{1,0:T(8,128)S(1)}, f32[656,128]{1,0:T(8,128)S(1)}, u32[]{:S(2)}, u32[]{:S(2)}) collective-permute-start(f32[656,128]{1,0:T(8,128)S(1)} %collective-permute-done.refs_0_), channel_id=1, source_target_pairs={{0,8},{1,9},{2,10},{3,11},{4,12},{5,13},{6,14},{7,15},{8,0},{9,1},... | collective-permute-start | bytes 1007624 | tf_op jit(solution)/shard_map/ppermute | solution.py:280
  49.2 1.6 %collective-permute-start.13 = (f32[656,128]{1,0:T(8,128)S(1)}, f32[656,128]{1,0:T(8,128)S(1)}, u32[]{:S(2)}, u32[]{:S(2)}) collective-permute-start(f32[656,128]{1,0:T(8,128)S(1)} %collective-permute-done.1.refs_1_), channel_id=1, source_target_pairs={{0,8},{1,9},{2,10},{3,11},{4,12},{5,13},{6,14},{7,15},{8,0},{9,1},... | collective-permute-start | bytes 1007624 | tf_op jit(solution)/shard_map/ppermute | solution.py:280
  54.6 2.0 %collective-permute-start.14 = (f32[4,128,256]{2,1,0:T(8,128)S(1)}, f32[4,128,256]{2,1,0:T(8,128)S(1)}, u32[]{:S(2)}, u32[]{:S(2)}) collective-permute-start(f32[4,128,256]{2,1,0:T(8,128)S(1)} %grad.3), channel_id=1, source_target_pairs={{0,8},{1,9},{2,10},{3,11},{4,12},{5,13},{6,14},{7,15},{8,0},{9,1},... | collective-permute-start | bytes 1572872 | tf_op jit(solution)/shard_map/ppermute | solution.py:280
  56.6 5.9 %collective-permute-start.15 = (f32[4,32,256]{2,1,0:T(8,128)S(1)}, f32[4,32,256]{2,1,0:T(8,128)S(1)}, u32[]{:S(2)}, u32[]{:S(2)}) collective-permute-start(f32[4,32,256]{2,1,0:T(8,128)S(1)} %get-tuple-element.47), channel_id=1, source_target_pairs={{0,16},{1,17},{2,18},{3,19},{4,20},{5,21},{6,22},{7,23},{8,24},{9,... | collective-permute-start | bytes 393224 | tf_op jit(solution)/shard_map/ppermute | solution.py:280
  58.2 8.1 %collective-permute-start.16 = (f32[4,32,256]{2,1,0:T(8,128)S(1)}, f32[4,32,256]{2,1,0:T(8,128)S(1)}, u32[]{:S(2)}, u32[]{:S(2)}) collective-permute-start(f32[4,32,256]{2,1,0:T(8,128)S(1)} %get-tuple-element.48), channel_id=1, source_target_pairs={{0,1},{1,0},{2,3},{3,2},{4,5},{5,4},{6,7},{7,6},{8,9},{9,8},{10,11... | collective-permute-start | bytes 393224 | tf_op jit(solution)/shard_map/ppermute | solution.py:280
  59.7 6.6 %collective-permute-start.17 = (f32[4,32,256]{2,1,0:T(8,128)S(1)}, f32[4,32,256]{2,1,0:T(8,128)S(1)}, u32[]{:S(2)}, u32[]{:S(2)}) collective-permute-start(f32[4,32,256]{2,1,0:T(8,128)S(1)} %get-tuple-element.49), channel_id=1, source_target_pairs={{0,17},{1,16},{2,19},{3,18},{4,21},{5,20},{6,23},{7,22},{8,25},{9,... | collective-permute-start | bytes 393224 | tf_op jit(solution)/shard_map/ppermute | solution.py:280
  66.3 4.2 %collective-permute-start.18 = (f32[32,256]{1,0:T(8,128)S(1)}, f32[32,256]{1,0:T(8,128)S(1)}, u32[]{:S(2)}, u32[]{:S(2)}) collective-permute-start(f32[32,256]{1,0:T(8,128)S(1)} %get-tuple-element.52), channel_id=1, source_target_pairs={{0,6},{1,7},{2,0},{3,1},{4,2},{5,3},{6,4},{7,5},{8,14},{9,15},{10,... | collective-permute-start | bytes 98312 | tf_op jit(solution)/shard_map/ppermute | solution.py:280
  68.0 5.0 %collective-permute-start.19 = (f32[32,256]{1,0:T(8,128)S(1)}, f32[32,256]{1,0:T(8,128)S(1)}, u32[]{:S(2)}, u32[]{:S(2)}) collective-permute-start(f32[32,256]{1,0:T(8,128)S(1)} %get-tuple-element.54), channel_id=1, source_target_pairs={{0,4},{1,5},{2,6},{3,7},{4,0},{5,1},{6,2},{7,3},{8,12},{9,13},{10,... | collective-permute-start | bytes 98312 | tf_op jit(solution)/shard_map/ppermute | solution.py:280
  68.0 5.7 %collective-permute-start.20 = (f32[32,256]{1,0:T(8,128)S(1)}, f32[32,256]{1,0:T(8,128)S(1)}, u32[]{:S(2)}, u32[]{:S(2)}) collective-permute-start(f32[32,256]{1,0:T(8,128)S(1)} %get-tuple-element.53), channel_id=1, source_target_pairs={{0,2},{1,3},{2,4},{3,5},{4,6},{5,7},{6,0},{7,1},{8,10},{9,11},{10,... | collective-permute-start | bytes 98312 | tf_op jit(solution)/shard_map/ppermute | solution.py:280
  73.7 3.3 %collective-permute-start.21 = (f32[32,256]{1,0:T(8,128)S(1)}, f32[32,256]{1,0:T(8,128)S(1)}, u32[]{:S(2)}, u32[]{:S(2)}) collective-permute-start(f32[32,256]{1,0:T(8,128)S(1)} %fusion.3.refs_0_), channel_id=1, source_target_pairs={{0,8},{1,9},{2,10},{3,11},{4,12},{5,13},{6,14},{7,15},{8,0},{9,1},... | collective-permute-start | bytes 98312 | tf_op jit(solution)/shard_map/ppermute | solution.py:280
  73.8 4.0 %collective-permute-start.22 = (f32[32,256]{1,0:T(8,128)S(1)}, f32[32,256]{1,0:T(8,128)S(1)}, u32[]{:S(2)}, u32[]{:S(2)}) collective-permute-start(f32[32,256]{1,0:T(8,128)S(1)} %fusion.3.refs_0_), channel_id=1, source_target_pairs={{0,16},{1,17},{2,18},{3,19},{4,20},{5,21},{6,22},{7,23},{8,24},{9,... | collective-permute-start | bytes 98312 | tf_op jit(solution)/shard_map/ppermute | solution.py:280
  75.1 3.3 %collective-permute-start.23 = (f32[32,256]{1,0:T(8,128)S(1)}, f32[32,256]{1,0:T(8,128)S(1)}, u32[]{:S(2)}, u32[]{:S(2)}) collective-permute-start(f32[32,256]{1,0:T(8,128)S(1)} %fusion.3.refs_0_), channel_id=1, source_target_pairs={{0,24},{1,25},{2,26},{3,27},{4,28},{5,29},{6,30},{7,31},{8,16},{9,... | collective-permute-start | bytes 98312 | tf_op jit(solution)/shard_map/ppermute | solution.py:280
  (5 other events, 6.0 us)

commit v4 on v3

--- a/solution.py
+++ b/solution.py
@@ -14,6 +14,7 @@
 NN = (((1,), (0,)), ((), ()))
 
 
+COST = pl.CostEstimate(flops=1, bytes_accessed=1, transcendentals=0)
 VMEM = pl.BlockSpec(memory_space=pltpu.VMEM)
 SMEM = pl.BlockSpec(memory_space=pltpu.SMEM)
 
@@ -31,7 +32,7 @@
     return lax.dot_general(a, b, dims, preferred_element_type=F32)
 
 
-def pack_kernel(parts, place_ref, cen_ref, coef_ref, width_ref, mine_ref, sib_ref, col_ref):
+def pack_kernel(parts, place_ref, cen_ref, coef_ref, width_ref, mine_ref, sib_ref, first_ref, col_ref):
     count, depth = cen_ref.shape
     piece = count // (2 * parts)
     blocks = depth // LANES
@@ -63,6 +64,7 @@
             out[(ahead + 1) * size - 8:(ahead + 1) * size, :] = tail
             inverse = jnp.concatenate([inverse[:, piece:], inverse[:, :piece]], axis=1)
             square = jnp.concatenate([square[:, piece:], square[:, :piece]], axis=1)
+    first_ref[...] = mine_ref[:size, :]
 
 
 def pack(place, centres, coefficients, widths, parts):
@@ -71,17 +73,18 @@
     rows = count // 2 * ((depth + width) // LANES) + 8 * parts
     shape = jax.ShapeDtypeStruct((rows, LANES), F32)
     out = pl.BlockSpec((rows, LANES), lambda i: (0, 0))
+    first = jax.ShapeDtypeStruct((rows // parts, LANES), F32)
     return pl.pallas_call(
         functools.partial(pack_kernel, parts),
         grid=(1,),
-        out_shape=(shape, shape),
+        out_shape=(shape, shape, first),
         in_specs=[
             SMEM,
             pl.BlockSpec((count, depth), lambda i: (0, 0)),
             pl.BlockSpec((count, width), lambda i: (0, 0)),
             pl.BlockSpec((1, count), lambda i: (0, 0)),
         ],
-        out_specs=(out, out),
+        out_specs=(out, out, pl.BlockSpec(first.shape, lambda i: (0, 0))),
         scratch_shapes=[pltpu.VMEM((count, LANES), F32)],
         compiler_params=params(),
         name="pack",
@@ -122,7 +125,7 @@
             pl.BlockSpec((width, step), lambda i: (0, i)),
         ),
         compiler_params=params(),
-        cost_estimate=pl.CostEstimate(flops=1, bytes_accessed=1, transcendentals=0),
+        cost_estimate=COST,
         name="prep",
     )(features, targets)
 
@@ -184,7 +187,7 @@
             pltpu.VMEM((count, LANES), F32),
         ],
         compiler_params=params(),
-        cost_estimate=pl.CostEstimate(flops=1, bytes_accessed=1, transcendentals=0),
+        cost_estimate=COST,
         name="plane",
     )(*messages, fh, fl, sq, acc)
 
@@ -210,7 +213,7 @@
         in_specs=[VMEM] * (1 + 2 * planes),
         out_specs=VMEM,
         compiler_params=params(),
-        cost_estimate=pl.CostEstimate(flops=1, bytes_accessed=1, transcendentals=0),
+        cost_estimate=COST,
         name="grad",
     )(acc, *khs, *kls)
 
@@ -279,26 +282,31 @@
                 pairs.append((g * owners + o, to * owners + ((o // 2 + k) % deep) * 2 + (o + y) % 2))
         return lax.ppermute(value, ("grp", "own"), pairs)
 
-    mine, sib = pack(place, centres, coefficients, widths.reshape(1, count), parts)
+    mine, sib, first = pack(place, centres, coefficients, widths.reshape(1, count), parts)
     order = sorted(range(1, deep), key=lambda k: min(k, deep - k))
+    shared = (deep // 2,)
     near = move(mine, y=1)
-    far = {k: move(mine, k=k) for k in order}
+    far = {k: move(first if k in shared else mine, k=k) for k in order}
     fh, fl, sq, acc = prep(features, targets, min(rows, 256))
-    messages = (mine, near, sib, move(near, core=1))
     khs, kls = {}, {}
-    khs[0], kls[0], acc = plane(messages, fh, fl, sq, acc, parts, piece)
-    accs = [sq,None,None]
-    others = {}
+    khs[0], kls[0], acc = plane((mine, near, sib, move(near, core=1)), fh, fl, sq, acc, parts, piece)
+    held = {}
     for n, k in enumerate(order):
-        same = after(far[k], accs[n]) if n < 3 and accs[n] is not None else far[k]
-        far[k] = same
-        others[k] = move(same, y=1)
+        same = after(far[k], sq) if n in (0,) else far[k]
+        if k in shared:
+            same = [same] + [move(same, ahead=-a) for a in range(1, parts)]
+            other = [move(same[0], y=1)]
+            for a in range(1, parts):
+                other.append(move(after(same[a], acc), y=1))
+            held[k] = same + other
+        else:
+            held[k] = [same, move(same, y=1)]
     for n, k in enumerate(order):
-        same, other = far[k], others[k]
-        if n==len(order)-1:
-            other = after(other, acc)
-        messages = (same, other, move(same, core=1), move(other, core=1))
-        khs[k], kls[k], acc = plane(messages, fh, fl, sq, acc, parts, piece)
+        pieces = held[k]
+        if n == len(order) - 1:
+            pieces[-1] = after(pieces[-1], acc)
+        pieces = pieces + [move(value, core=1) for value in pieces]
+        khs[k], kls[k], acc = plane(pieces, fh, fl, sq, acc, parts, piece)
     khs = [khs[k] for k in range(deep)]
     kls = [kls[k] for k in range(deep)]
 

time: 79.9 us -> 78.2 us (0.979)
  waiting for transfers between devices: 25 us -> 18.4 us
  starting transfers between devices: 30.5 us -> 35.3 us
    ppermute x24 -> x28, waiting for transfers between devices: 25 us -> 18.4 us  [move(): return lax.ppermute(value, ('grp', 'own'), pairs)]
    ppermute x24 -> x28, starting transfers between devices: 30.5 us -> 35.3 us  [move(): return lax.ppermute(value, ('grp', 'own'), pairs)]
  transfers between devices with their start and end apart: 24 -> 28, of which waited for: 12 -> 10; matrix products, arithmetic and copies ran while one was open for 2% -> 2% of each run, Pallas kernels for 13% -> 13%
where the time goes in v4:
time: 78.2 us; the launch traced here: 77.9 us
  starting transfers between devices  35.3 us (45%)
  waiting for transfers between devices  18.4 us (24%)
  Pallas kernels  16 us (20%)
  local copies, waits for them, and re-layouts  7.33 us (9%)
  between operations  0.79 us (1%)
    ppermute x28, starting transfers between devices, move(): return lax.ppermute(value, ('grp', 'own'), pairs)  35.3 us
    ppermute x28, waiting for transfers between devices, move(): return lax.ppermute(value, ('grp', 'own'), pairs)  18.4 us
    pallas_call x4, Pallas kernels, plane(): pl.pallas_call(functools.partial(plane_kernel, parts, len(messages), piec...  9.63 us
    unnamed x11, local copies, waits for them, and re-layouts  7.32 us
    pallas_call x2, Pallas kernels, grad(): pl.pallas_call(functools.partial(grad_kernel, planes, which), out_shape=j...  2.73 us
  transfers between devices with their start and end apart: 28, of which 10 were waited for; matrix products, arithmetic and copies ran while one was open for 2% of the time, Pallas kernels for 13%

profile of v4, /device:TPU:0, one launch (start us, length us, event | category | flops | bytes accessed | tf_op | source)
XLA Modules:
  0.0 77.9 jit_solution(11596052556024364433)
XLA Ops:
  4.2 3.0 %collective-permute-start.10 = (f32[656,128]{1,0:T(8,128)S(1)}, f32[656,128]{1,0:T(8,128)S(1)}, u32[]{:S(2)}, u32[]{:S(2)}) collective-permute-start(f32[656,128]{1,0:T(8,128)S(1)} %get-tuple-element.29.refs_0_), channel_id=1, source_target_pairs={{0,2},{1,3},{2,4},{3,5},{4,6},{5,7},{6,0},{7,1},{8,10},{9,11},{10,... | collective-permute-start | bytes 1007624 | tf_op jit(solution)/shard_map/ppermute | solution.py:283
  7.3 2.0 %collective-permute-start.6 = (f32[656,128]{1,0:T(8,128)S(1)}, f32[656,128]{1,0:T(8,128)S(1)}, u32[]{:S(2)}, u32[]{:S(2)}) collective-permute-start(f32[656,128]{1,0:T(8,128)S(1)} %get-tuple-element.29.refs_0_), channel_id=1, source_target_pairs={{0,6},{1,7},{2,0},{3,1},{4,2},{5,3},{6,4},{7,5},{8,14},{9,15},{10,... | collective-permute-start | bytes 1007624 | tf_op jit(solution)/shard_map/ppermute | solution.py:283
  9.3 1.7 %collective-permute-start.3 = (f32[656,128]{1,0:T(8,128)S(1)}, f32[656,128]{1,0:T(8,128)S(1)}, u32[]{:S(2)}, u32[]{:S(2)}) collective-permute-start(f32[656,128]{1,0:T(8,128)S(1)} %get-tuple-element.29.refs_0_), channel_id=1, source_target_pairs={{0,1},{1,0},{2,3},{3,2},{4,5},{5,4},{6,7},{7,6},{8,9},{9,8},{10,11... | collective-permute-start | bytes 1007624 | tf_op jit(solution)/shard_map/ppermute | solution.py:283
  11.1 2.2 %copy-done = f32[1024,1024]{1,0:T(8,128)S(1)} copy-done((f32[1024,1024]{1,0:T(8,128)S(1)}, f32[1024,1024]{1,0:T(8,128)}, u32[]{:S(2)}) %copy-start) | copy-done | bytes 4194328
  14.5 1.5 %prep.1 = (bf16[1024,1024]{1,0:T(8,128)(2,1)S(1)}, bf16[1024,1024]{1,0:T(8,128)(2,1)S(1)}, f32[8,1024]{1,0:T(8,128)S(1)}, f32[256,1024]{1,0:T(8,128)S(1)}) custom-call(f32[1024,1024]{1,0:T(8,128)S(1)} %copy-done, f32[1024,256]{1,0:T(8,128)S(1)} %copy-done.1), custom_call_target="tpu_custom_call" | custom-call | flops 1 | bytes 1 | tf_op jit(solution)/shard_map/prep/pallas_call | solution.py:111
  15.9 2.1 %collective-permute-done.10.refs_0_ = f32[656,128]{1,0:T(8,128)S(1)} collective-permute-done((f32[656,128]{1,0:T(8,128)S(1)}, f32[656,128]{1,0:T(8,128)S(1)}, u32[]{:S(2)}, u32[]{:S(2)}) %collective-permute-start.10) | collective-permute-done | bytes 335904 | tf_op jit(solution)/shard_map/ppermute | solution.py:283
  18.1 1.8 %collective-permute-start.11 = (f32[656,128]{1,0:T(8,128)S(1)}, f32[656,128]{1,0:T(8,128)S(1)}, u32[]{:S(2)}, u32[]{:S(2)}) collective-permute-start(f32[656,128]{1,0:T(8,128)S(1)} %collective-permute-done.10.refs_0_), channel_id=1, source_target_pairs={{0,1},{1,0},{2,3},{3,2},{4,5},{5,4},{6,7},{7,6},{8,9},{9,8},{10,11... | collective-permute-start | bytes 1007624 | tf_op jit(solution)/shard_map/ppermute | solution.py:283
  19.8 8.6 %collective-permute-start = (f32[328,128]{1,0:T(8,128)S(1)}, f32[328,128]{1,0:T(8,128)S(1)}, u32[]{:S(2)}, u32[]{:S(2)}) collective-permute-start(f32[328,128]{1,0:T(8,128)S(1)} %get-tuple-element.28), channel_id=1, source_target_pairs={{0,4},{1,5},{2,6},{3,7},{4,0},{5,1},{6,2},{7,3},{8,12},{9,13},{10,... | collective-permute-start | bytes 503816 | tf_op jit(solution)/shard_map/ppermute | solution.py:283
  29.0 2.8 %collective-permute-done.refs_0_ = f32[328,128]{1,0:T(8,128)S(1)} collective-permute-done((f32[328,128]{1,0:T(8,128)S(1)}, f32[328,128]{1,0:T(8,128)S(1)}, u32[]{:S(2)}, u32[]{:S(2)}) %collective-permute-start) | collective-permute-done | bytes 167968 | tf_op jit(solution)/shard_map/ppermute | solution.py:283
  31.8 1.5 %collective-permute-start.1 = (f32[328,128]{1,0:T(8,128)S(1)}, f32[328,128]{1,0:T(8,128)S(1)}, u32[]{:S(2)}, u32[]{:S(2)}) collective-permute-start(f32[328,128]{1,0:T(8,128)S(1)} %collective-permute-done.refs_0_), channel_id=1, source_target_pairs={{0,16},{1,17},{2,18},{3,19},{4,20},{5,21},{6,22},{7,23},{8,24},{9,... | collective-permute-start | bytes 503816 | tf_op jit(solution)/shard_map/ppermute | solution.py:283
  33.8 3.4 %collective-permute-done.1.refs_1_ = f32[328,128]{1,0:T(8,128)S(1)} collective-permute-done((f32[328,128]{1,0:T(8,128)S(1)}, f32[328,128]{1,0:T(8,128)S(1)}, u32[]{:S(2)}, u32[]{:S(2)}) %collective-permute-start.1) | collective-permute-done | bytes 167968 | tf_op jit(solution)/shard_map/ppermute | solution.py:283
  37.7 1.3 %collective-permute-start.2 = (f32[328,128]{1,0:T(8,128)S(1)}, f32[328,128]{1,0:T(8,128)S(1)}, u32[]{:S(2)}, u32[]{:S(2)}) collective-permute-start(f32[328,128]{1,0:T(8,128)S(1)} %collective-permute-done.refs_0_), channel_id=1, source_target_pairs={{0,1},{1,0},{2,3},{3,2},{4,5},{5,4},{6,7},{7,6},{8,9},{9,8},{10,11... | collective-permute-start | bytes 503816 | tf_op jit(solution)/shard_map/ppermute | solution.py:283
  39.0 2.4 %plane.4 = (bf16[256,1024]{1,0:T(8,128)(2,1)S(1)}, bf16[256,1024]{1,0:T(8,128)(2,1)S(1)}, f32[256,1024]{1,0:T(8,128)S(1)}) custom-call(f32[656,128]{1,0:T(8,128)S(1)} %get-tuple-element.29.refs_0_, f32[656,128]{1,0:T(8,128)S(1)} %collective-permute-done.3.refs_1_, f32[656,128]{1,0:T(8,128)S(1)} %get-tuple-element.30.refs_2_, ...), custom_call_target="tpu_custom_call" | custom-call | flops 1 | bytes 1 | tf_op jit(solution)/shard_map/plane/pallas_call | solution.py:173
  42.2 2.4 %plane.5 = (bf16[256,1024]{1,0:T(8,128)(2,1)S(1)}, bf16[256,1024]{1,0:T(8,128)(2,1)S(1)}, f32[256,1024]{1,0:T(8,128)S(1)}) custom-call(f32[656,128]{1,0:T(8,128)S(1)} %collective-permute-done.10.refs_0_, f32[656,128]{1,0:T(8,128)S(1)} %collective-permute-done.11.refs_1_, f32[656,128]{1,0:T(8,128)S(1)} %collective-permute-done.12.refs_2_, ...), custom_call_target="tpu_custom_call" | custom-call | flops 1 | bytes 1 | tf_op jit(solution)/shard_map/plane/pallas_call | solution.py:173
  45.3 2.4 %plane.6 = (bf16[256,1024]{1,0:T(8,128)(2,1)S(1)}, bf16[256,1024]{1,0:T(8,128)(2,1)S(1)}, f32[256,1024]{1,0:T(8,128)S(1)}) custom-call(f32[656,128]{1,0:T(8,128)S(1)} %collective-permute-done.6.refs_0_, f32[656,128]{1,0:T(8,128)S(1)} %collective-permute-done.7.refs_1_, f32[656,128]{1,0:T(8,128)S(1)} %collective-permute-done.8.refs_2_, ...), custom_call_target="tpu_custom_call" | custom-call | flops 1 | bytes 1 | tf_op jit(solution)/shard_map/plane/pallas_call | solution.py:173
  49.2 2.4 %plane.7 = (bf16[256,1024]{1,0:T(8,128)(2,1)S(1)}, bf16[256,1024]{1,0:T(8,128)(2,1)S(1)}, f32[256,1024]{1,0:T(8,128)S(1)}) custom-call(f32[328,128]{1,0:T(8,128)S(1)} %collective-permute-done.refs_0_, f32[328,128]{1,0:T(8,128)S(1)} %collective-permute-done.1.refs_1_, f32[328,128]{1,0:T(8,128)S(1)} %collective-permute-done.2.refs_2_, ...), custom_call_target="tpu_custom_call" | custom-call | flops 1 | bytes 1 | tf_op jit(solution)/shard_map/plane/pallas_call | solution.py:173
  51.6 1.4 %grad.3 = f32[4,128,256]{2,1,0:T(8,128)S(1)} custom-call(f32[256,1024]{1,0:T(8,128)S(1)} %get-tuple-element.41.acc_ref, bf16[256,1024]{1,0:T(8,128)(2,1)S(1)} %get-tuple-element.42.refs_0_, bf16[256,1024]{1,0:T(8,128)(2,1)S(1)} %get-tuple-element.43.refs_1_, bf16[256,1024]{1,0:T(8,128)(2,1)S(1)} %get-tuple-element.44.refs_2_, ...), custom_call_target="tpu_custom_call" | custom-call | flops 1 | bytes 1 | tf_op jit(solution)/shard_map/grad/pallas_call | solution.py:210
  53.5 1.4 %grad.2.kept_ref = f32[4,128,256]{2,1,0:T(8,128)S(1)} custom-call(f32[256,1024]{1,0:T(8,128)S(1)} %get-tuple-element.41.acc_ref, bf16[256,1024]{1,0:T(8,128)(2,1)S(1)} %get-tuple-element.42.refs_0_, bf16[256,1024]{1,0:T(8,128)(2,1)S(1)} %get-tuple-element.43.refs_1_, bf16[256,1024]{1,0:T(8,128)(2,1)S(1)} %get-tuple-element.44.refs_2_, ...), custom_call_target="tpu_custom_call" | custom-call | flops 1 | bytes 1 | tf_op jit(solution)/shard_map/grad/pallas_call | solution.py:210
  55.1 2.3 %collective-permute-start.21 = (f32[4,32,256]{2,1,0:T(8,128)S(1)}, f32[4,32,256]{2,1,0:T(8,128)S(1)}, u32[]{:S(2)}, u32[]{:S(2)}) collective-permute-start(f32[4,32,256]{2,1,0:T(8,128)S(1)} %get-tuple-element.53), channel_id=1, source_target_pairs={{0,17},{1,16},{2,19},{3,18},{4,21},{5,20},{6,23},{7,22},{8,25},{9,... | collective-permute-start | bytes 393224 | tf_op jit(solution)/shard_map/ppermute | solution.py:283
  58.6 3.6 %collective-permute-done.21 = f32[4,32,256]{2,1,0:T(8,128)S(1)} collective-permute-done((f32[4,32,256]{2,1,0:T(8,128)S(1)}, f32[4,32,256]{2,1,0:T(8,128)S(1)}, u32[]{:S(2)}, u32[]{:S(2)}) %collective-permute-start.21) | collective-permute-done | bytes 131104 | tf_op jit(solution)/shard_map/ppermute | solution.py:283
  62.3 2.3 %collective-permute-done.20 = f32[4,32,256]{2,1,0:T(8,128)S(1)} collective-permute-done((f32[4,32,256]{2,1,0:T(8,128)S(1)}, f32[4,32,256]{2,1,0:T(8,128)S(1)}, u32[]{:S(2)}, u32[]{:S(2)}) %collective-permute-start.20) | collective-permute-done | bytes 131104 | tf_op jit(solution)/shard_map/ppermute | solution.py:283
  64.7 3.0 %collective-permute-start.23 = (f32[32,256]{1,0:T(8,128)S(1)}, f32[32,256]{1,0:T(8,128)S(1)}, u32[]{:S(2)}, u32[]{:S(2)}) collective-permute-start(f32[32,256]{1,0:T(8,128)S(1)} %get-tuple-element.58), channel_id=1, source_target_pairs={{0,4},{1,5},{2,6},{3,7},{4,0},{5,1},{6,2},{7,3},{8,12},{9,13},{10,... | collective-permute-start | bytes 98312 | tf_op jit(solution)/shard_map/ppermute | solution.py:283
  67.7 2.8 %collective-permute-start.22 = (f32[32,256]{1,0:T(8,128)S(1)}, f32[32,256]{1,0:T(8,128)S(1)}, u32[]{:S(2)}, u32[]{:S(2)}) collective-permute-start(f32[32,256]{1,0:T(8,128)S(1)} %get-tuple-element.56), channel_id=1, source_target_pairs={{0,6},{1,7},{2,0},{3,1},{4,2},{5,3},{6,4},{7,5},{8,14},{9,15},{10,... | collective-permute-start | bytes 98312 | tf_op jit(solution)/shard_map/ppermute | solution.py:283
  70.6 1.6 %collective-permute-done.22 = f32[32,256]{1,0:T(8,128)S(1)} collective-permute-done((f32[32,256]{1,0:T(8,128)S(1)}, f32[32,256]{1,0:T(8,128)S(1)}, u32[]{:S(2)}, u32[]{:S(2)}) %collective-permute-start.22) | collective-permute-done | bytes 32800 | tf_op jit(solution)/shard_map/ppermute | solution.py:283
  (57 shorter events, 17.1 us)
Async XLA Ops:
  4.2 13.8 %collective-permute-start.10 = (f32[656,128]{1,0:T(8,128)S(1)}, f32[656,128]{1,0:T(8,128)S(1)}, u32[]{:S(2)}, u32[]{:S(2)}) collective-permute-start(f32[656,128]{1,0:T(8,128)S(1)} %get-tuple-element.29.refs_0_), channel_id=1, source_target_pairs={{0,2},{1,3},{2,4},{3,5},{4,6},{5,7},{6,0},{7,1},{8,10},{9,11},{10,... | collective-permute-start | bytes 1007624 | tf_op jit(solution)/shard_map/ppermute | solution.py:283
  7.3 21.2 %collective-permute-start.6 = (f32[656,128]{1,0:T(8,128)S(1)}, f32[656,128]{1,0:T(8,128)S(1)}, u32[]{:S(2)}, u32[]{:S(2)}) collective-permute-start(f32[656,128]{1,0:T(8,128)S(1)} %get-tuple-element.29.refs_0_), channel_id=1, source_target_pairs={{0,6},{1,7},{2,0},{3,1},{4,2},{5,3},{6,4},{7,5},{8,14},{9,15},{10,... | collective-permute-start | bytes 1007624 | tf_op jit(solution)/shard_map/ppermute | solution.py:283
  9.3 19.6 %collective-permute-start.3 = (f32[656,128]{1,0:T(8,128)S(1)}, f32[656,128]{1,0:T(8,128)S(1)}, u32[]{:S(2)}, u32[]{:S(2)}) collective-permute-start(f32[656,128]{1,0:T(8,128)S(1)} %get-tuple-element.29.refs_0_), channel_id=1, source_target_pairs={{0,1},{1,0},{2,3},{3,2},{4,5},{5,4},{6,7},{7,6},{8,9},{9,8},{10,11... | collective-permute-start | bytes 1007624 | tf_op jit(solution)/shard_map/ppermute | solution.py:283
  18.1 15.2 %collective-permute-start.11 = (f32[656,128]{1,0:T(8,128)S(1)}, f32[656,128]{1,0:T(8,128)S(1)}, u32[]{:S(2)}, u32[]{:S(2)}) collective-permute-start(f32[656,128]{1,0:T(8,128)S(1)} %collective-permute-done.10.refs_0_), channel_id=1, source_target_pairs={{0,1},{1,0},{2,3},{3,2},{4,5},{5,4},{6,7},{7,6},{8,9},{9,8},{10,11... | collective-permute-start | bytes 1007624 | tf_op jit(solution)/shard_map/ppermute | solution.py:283
  19.8 11.9 %collective-permute-start = (f32[328,128]{1,0:T(8,128)S(1)}, f32[328,128]{1,0:T(8,128)S(1)}, u32[]{:S(2)}, u32[]{:S(2)}) collective-permute-start(f32[328,128]{1,0:T(8,128)S(1)} %get-tuple-element.28), channel_id=1, source_target_pairs={{0,4},{1,5},{2,6},{3,7},{4,0},{5,1},{6,2},{7,3},{8,12},{9,13},{10,... | collective-permute-start | bytes 503816 | tf_op jit(solution)/shard_map/ppermute | solution.py:283
  28.4 8.7 %collective-permute-start.7 = (f32[656,128]{1,0:T(8,128)S(1)}, f32[656,128]{1,0:T(8,128)S(1)}, u32[]{:S(2)}, u32[]{:S(2)}) collective-permute-start(f32[656,128]{1,0:T(8,128)S(1)} %collective-permute-done.6.refs_0_), channel_id=1, source_target_pairs={{0,1},{1,0},{2,3},{3,2},{4,5},{5,4},{6,7},{7,6},{8,9},{9,8},{10,11... | collective-permute-start | bytes 1007624 | tf_op jit(solution)/shard_map/ppermute | solution.py:283
  29.0 8.7 %collective-permute-start.4 = (f32[656,128]{1,0:T(8,128)S(1)}, f32[656,128]{1,0:T(8,128)S(1)}, u32[]{:S(2)}, u32[]{:S(2)}) collective-permute-start(f32[656,128]{1,0:T(8,128)S(1)} %collective-permute-done.3.refs_1_), channel_id=1, source_target_pairs={{0,8},{1,9},{2,10},{3,11},{4,12},{5,13},{6,14},{7,15},{8,0},{9,1},... | collective-permute-start | bytes 1007624 | tf_op jit(solution)/shard_map/ppermute | solution.py:283
  31.8 5.4 %collective-permute-start.1 = (f32[328,128]{1,0:T(8,128)S(1)}, f32[328,128]{1,0:T(8,128)S(1)}, u32[]{:S(2)}, u32[]{:S(2)}) collective-permute-start(f32[328,128]{1,0:T(8,128)S(1)} %collective-permute-done.refs_0_), channel_id=1, source_target_pairs={{0,16},{1,17},{2,18},{3,19},{4,20},{5,21},{6,22},{7,23},{8,24},{9,... | collective-permute-start | bytes 503816 | tf_op jit(solution)/shard_map/ppermute | solution.py:283
  33.3 8.1 %collective-permute-start.12 = (f32[656,128]{1,0:T(8,128)S(1)}, f32[656,128]{1,0:T(8,128)S(1)}, u32[]{:S(2)}, u32[]{:S(2)}) collective-permute-start(f32[656,128]{1,0:T(8,128)S(1)} %collective-permute-done.10.refs_0_), channel_id=1, source_target_pairs={{0,8},{1,9},{2,10},{3,11},{4,12},{5,13},{6,14},{7,15},{8,0},{9,1},... | collective-permute-start | bytes 1007624 | tf_op jit(solution)/shard_map/ppermute | solution.py:283
  33.3 8.9 %collective-permute-start.13 = (f32[656,128]{1,0:T(8,128)S(1)}, f32[656,128]{1,0:T(8,128)S(1)}, u32[]{:S(2)}, u32[]{:S(2)}) collective-permute-start(f32[656,128]{1,0:T(8,128)S(1)} %collective-permute-done.11.refs_1_), channel_id=1, source_target_pairs={{0,8},{1,9},{2,10},{3,11},{4,12},{5,13},{6,14},{7,15},{8,0},{9,1},... | collective-permute-start | bytes 1007624 | tf_op jit(solution)/shard_map/ppermute | solution.py:283
  37.1 8.0 %collective-permute-start.8 = (f32[656,128]{1,0:T(8,128)S(1)}, f32[656,128]{1,0:T(8,128)S(1)}, u32[]{:S(2)}, u32[]{:S(2)}) collective-permute-start(f32[656,128]{1,0:T(8,128)S(1)} %collective-permute-done.6.refs_0_), channel_id=1, source_target_pairs={{0,8},{1,9},{2,10},{3,11},{4,12},{5,13},{6,14},{7,15},{8,0},{9,1},... | collective-permute-start | bytes 1007624 | tf_op jit(solution)/shard_map/ppermute | solution.py:283
  37.1 8.1 %collective-permute-start.9 = (f32[656,128]{1,0:T(8,128)S(1)}, f32[656,128]{1,0:T(8,128)S(1)}, u32[]{:S(2)}, u32[]{:S(2)}) collective-permute-start(f32[656,128]{1,0:T(8,128)S(1)} %collective-permute-done.7.refs_1_), channel_id=1, source_target_pairs={{0,8},{1,9},{2,10},{3,11},{4,12},{5,13},{6,14},{7,15},{8,0},{9,1},... | collective-permute-start | bytes 1007624 | tf_op jit(solution)/shard_map/ppermute | solution.py:283
  37.7 6.9 %collective-permute-start.2 = (f32[328,128]{1,0:T(8,128)S(1)}, f32[328,128]{1,0:T(8,128)S(1)}, u32[]{:S(2)}, u32[]{:S(2)}) collective-permute-start(f32[328,128]{1,0:T(8,128)S(1)} %collective-permute-done.refs_0_), channel_id=1, source_target_pairs={{0,1},{1,0},{2,3},{3,2},{4,5},{5,4},{6,7},{7,6},{8,9},{9,8},{10,11... | collective-permute-start | bytes 503816 | tf_op jit(solution)/shard_map/ppermute | solution.py:283
  41.4 6.3 %collective-permute-start.5 = (f32[328,128]{1,0:T(8,128)S(1)}, f32[328,128]{1,0:T(8,128)S(1)}, u32[]{:S(2)}, u32[]{:S(2)}) collective-permute-start(f32[328,128]{1,0:T(8,128)S(1)} %collective-permute-done.1.refs_1_), channel_id=1, source_target_pairs={{0,1},{1,0},{2,3},{3,2},{4,5},{5,4},{6,7},{7,6},{8,9},{9,8},{10,11... | collective-permute-start | bytes 503816 | tf_op jit(solution)/shard_map/ppermute | solution.py:283
  42.2 6.0 %collective-permute-start.14 = (f32[328,128]{1,0:T(8,128)S(1)}, f32[328,128]{1,0:T(8,128)S(1)}, u32[]{:S(2)}, u32[]{:S(2)}) collective-permute-start(f32[328,128]{1,0:T(8,128)S(1)} %collective-permute-done.refs_0_), channel_id=1, source_target_pairs={{0,8},{1,9},{2,10},{3,11},{4,12},{5,13},{6,14},{7,15},{8,0},{9,1},... | collective-permute-start | bytes 503816 | tf_op jit(solution)/shard_map/ppermute | solution.py:283
  44.6 3.6 %collective-permute-start.15 = (f32[328,128]{1,0:T(8,128)S(1)}, f32[328,128]{1,0:T(8,128)S(1)}, u32[]{:S(2)}, u32[]{:S(2)}) collective-permute-start(f32[328,128]{1,0:T(8,128)S(1)} %collective-permute-done.1.refs_1_), channel_id=1, source_target_pairs={{0,8},{1,9},{2,10},{3,11},{4,12},{5,13},{6,14},{7,15},{8,0},{9,1},... | collective-permute-start | bytes 503816 | tf_op jit(solution)/shard_map/ppermute | solution.py:283
  55.1 7.2 %collective-permute-start.21 = (f32[4,32,256]{2,1,0:T(8,128)S(1)}, f32[4,32,256]{2,1,0:T(8,128)S(1)}, u32[]{:S(2)}, u32[]{:S(2)}) collective-permute-start(f32[4,32,256]{2,1,0:T(8,128)S(1)} %get-tuple-element.53), channel_id=1, source_target_pairs={{0,17},{1,16},{2,19},{3,18},{4,21},{5,20},{6,23},{7,22},{8,25},{9,... | collective-permute-start | bytes 393224 | tf_op jit(solution)/shard_map/ppermute | solution.py:283
  57.4 7.2 %collective-permute-start.20 = (f32[4,32,256]{2,1,0:T(8,128)S(1)}, f32[4,32,256]{2,1,0:T(8,128)S(1)}, u32[]{:S(2)}, u32[]{:S(2)}) collective-permute-start(f32[4,32,256]{2,1,0:T(8,128)S(1)} %get-tuple-element.52), channel_id=1, source_target_pairs={{0,1},{1,0},{2,3},{3,2},{4,5},{5,4},{6,7},{7,6},{8,9},{9,8},{10,11... | collective-permute-start | bytes 393224 | tf_op jit(solution)/shard_map/ppermute | solution.py:283
  58.1 6.5 %collective-permute-start.19 = (f32[4,32,256]{2,1,0:T(8,128)S(1)}, f32[4,32,256]{2,1,0:T(8,128)S(1)}, u32[]{:S(2)}, u32[]{:S(2)}) collective-permute-start(f32[4,32,256]{2,1,0:T(8,128)S(1)} %get-tuple-element.51), channel_id=1, source_target_pairs={{0,16},{1,17},{2,18},{3,19},{4,20},{5,21},{6,22},{7,23},{8,24},{9,... | collective-permute-start | bytes 393224 | tf_op jit(solution)/shard_map/ppermute | solution.py:283
  64.7 5.9 %collective-permute-start.24 = (f32[32,256]{1,0:T(8,128)S(1)}, f32[32,256]{1,0:T(8,128)S(1)}, u32[]{:S(2)}, u32[]{:S(2)}) collective-permute-start(f32[32,256]{1,0:T(8,128)S(1)} %get-tuple-element.57), channel_id=1, source_target_pairs={{0,2},{1,3},{2,4},{3,5},{4,6},{5,7},{6,0},{7,1},{8,10},{9,11},{10,... | collective-permute-start | bytes 98312 | tf_op jit(solution)/shard_map/ppermute | solution.py:283
  64.7 5.8 %collective-permute-start.23 = (f32[32,256]{1,0:T(8,128)S(1)}, f32[32,256]{1,0:T(8,128)S(1)}, u32[]{:S(2)}, u32[]{:S(2)}) collective-permute-start(f32[32,256]{1,0:T(8,128)S(1)} %get-tuple-element.58), channel_id=1, source_target_pairs={{0,4},{1,5},{2,6},{3,7},{4,0},{5,1},{6,2},{7,3},{8,12},{9,13},{10,... | collective-permute-start | bytes 98312 | tf_op jit(solution)/shard_map/ppermute | solution.py:283
  67.7 4.4 %collective-permute-start.22 = (f32[32,256]{1,0:T(8,128)S(1)}, f32[32,256]{1,0:T(8,128)S(1)}, u32[]{:S(2)}, u32[]{:S(2)}) collective-permute-start(f32[32,256]{1,0:T(8,128)S(1)} %get-tuple-element.56), channel_id=1, source_target_pairs={{0,6},{1,7},{2,0},{3,1},{4,2},{5,3},{6,4},{7,5},{8,14},{9,15},{10,... | collective-permute-start | bytes 98312 | tf_op jit(solution)/shard_map/ppermute | solution.py:283
  72.2 4.1 %collective-permute-start.26 = (f32[32,256]{1,0:T(8,128)S(1)}, f32[32,256]{1,0:T(8,128)S(1)}, u32[]{:S(2)}, u32[]{:S(2)}) collective-permute-start(f32[32,256]{1,0:T(8,128)S(1)} %fusion.3.refs_0_), channel_id=1, source_target_pairs={{0,16},{1,17},{2,18},{3,19},{4,20},{5,21},{6,22},{7,23},{8,24},{9,... | collective-permute-start | bytes 98312 | tf_op jit(solution)/shard_map/ppermute | solution.py:283
  73.1 3.6 %collective-permute-start.27 = (f32[32,256]{1,0:T(8,128)S(1)}, f32[32,256]{1,0:T(8,128)S(1)}, u32[]{:S(2)}, u32[]{:S(2)}) collective-permute-start(f32[32,256]{1,0:T(8,128)S(1)} %fusion.3.refs_0_), channel_id=1, source_target_pairs={{0,24},{1,25},{2,26},{3,27},{4,28},{5,29},{6,30},{7,31},{8,16},{9,... | collective-permute-start | bytes 98312 | tf_op jit(solution)/shard_map/ppermute | solution.py:283
  (9 other events, 15.8 us)
